TPU v7x, 32 devices: a whole 2x2x4 slice. The times are simulated.
32 devices in a mesh: dp: 8 (over z, core), fsdp: 4 (over y, x).
Axes of the slice: x: 2, y: 2, z: 4, core: 2. Of those that a mesh axis runs over, the one named last changes fastest.
Arguments:
- tokens: bfloat16 [16384, 1024], P(('dp', 'fsdp')), may hold values from -6 to 6
- segments: int32 [16384], P(('dp', 'fsdp')), may hold values from 0 to 127, as said below
- cotangent: bfloat16 [16384, 1024], P(('dp', 'fsdp')), may hold values from -6 to 6
- attn_w: float32 [4, 1024, 1024], P(None, 'dp', 'fsdp'), may hold values from -1.5 to 1.5
- ffn_w: float32 [2, 1024, 4096], P(None, 'dp', 'fsdp'), may hold values from -0.1875 to 0.1875
- vectors: float32 [12, 1024], P(None, ('dp', 'fsdp')), may hold values from -1.2 to 1.4
- attn_mom: float32 [4, 1024, 1024], P(None, 'dp', 'fsdp'), may hold values from -768 to 768
- ffn_mom: float32 [2, 1024, 4096], P(None, 'dp', 'fsdp'), may hold values from -896 to 896
- vec_mom: float32 [12, 1024], P(None, ('dp', 'fsdp')), may hold values from -230.4 to 230.4
- attn_ema: float32 [4, 1024, 1024], P(None, 'dp', 'fsdp'), may hold values from -1.5 to 1.5
- ffn_ema: float32 [2, 1024, 4096], P(None, 'dp', 'fsdp'), may hold values from -0.1875 to 0.1875
- vec_ema: float32 [12, 1024], P(None, ('dp', 'fsdp')), may hold values from -1.2 to 1.4
Outputs:
- layer_out: bfloat16 [16384, 1024], P(('dp', 'fsdp'))
- input_grad: float32 [16384, 1024], P(('dp', 'fsdp'))
- attn_new: float32 [4, 1024, 1024], P(None, 'dp', 'fsdp')
- ffn_new: float32 [2, 1024, 4096], P(None, 'dp', 'fsdp')
- vec_new: float32 [12, 1024], P(None, ('dp', 'fsdp'))
- attn_mom_new: float32 [4, 1024, 1024], P(None, 'dp', 'fsdp')
- ffn_mom_new: float32 [2, 1024, 4096], P(None, 'dp', 'fsdp')
- vec_mom_new: float32 [12, 1024], P(None, ('dp', 'fsdp'))
- attn_ema_new: float32 [4, 1024, 1024], P(None, 'dp', 'fsdp')
- ffn_ema_new: float32 [2, 1024, 4096], P(None, 'dp', 'fsdp')
- vec_ema_new: float32 [12, 1024], P(None, ('dp', 'fsdp'))
- out_bias_grad: float32 [1024], P(('dp', 'fsdp'))
Inputs may be any that keep to these rules, and one draw needn't show every extreme that they name: `segments`: each aligned block of 512 positions holds either one item or four items of 128 positions, and the last block four; ids never fall along the positions and differ between items.
All inputs are finite; a program needn't handle non-finite values.
Results may differ from a plain program's by a relative error of at most 0.035.
Values may be sent and summed in bfloat16 or wider, within the bound.
A program may use at most 256 MiB of HBM per device.

v0:
```python
import functools
import math

import jax
import jax.numpy as jnp
from jax import lax
from jax.experimental import pallas as pl
from jax.experimental.pallas import tpu as pltpu
from jax.sharding import PartitionSpec as P

D = 1024
FF = 4096
HEADS = 16
HDIM = 64
TILE = 512
ITERS = 5


score_scale = 0.125
ln_epsilon = 1e-05
norm_epsilon = 1e-06
ns_linear = 3.4445
ns_square = -4.775
ns_cubic = 2.0315
matrix_decay = 0.95
vector_decay = 0.9
average_decay = 0.7
weight_decay = 0.01
attn_rates = (1.0, 1.0, 1.0, 10.0)
vector_step = 0.3


def product(left, right):
    return jnp.dot(left, right, preferred_element_type=jnp.float32)


def contract_rows(left, right):
    return lax.dot_general(
        left, right, (((0,), (0,)), ((), ())), preferred_element_type=jnp.float32
    )


def contract_cols(left, right):
    return lax.dot_general(
        left, right, (((1,), (1,)), ((), ())), preferred_element_type=jnp.float32
    )


MESH = pl.DeviceIdType.MESH
ROLES = 8
STEP_ROWS = 512
NORM_ROWS = 128
TILE_ROWS = 128


def greet(partners):
    barrier = pltpu.get_barrier_semaphore()
    for partner in partners:
        pl.semaphore_signal(barrier, inc=1, device_id=partner, device_id_type=MESH)
    pl.semaphore_wait(barrier, len(partners))


def place(ndp, nf):
    dp, fs = lax.axis_index("dp"), lax.axis_index("fsdp")
    side = math.isqrt(nf)
    return lax.div(dp, 2), lax.rem(dp, 2), lax.div(fs, side), lax.rem(fs, side), ndp // 2, side


def line_partners(ndp, nf):
    z, core, y, x, nz, side = place(ndp, nf)
    mine = y * side + x
    return (
        [(z * 2 + 1 - core, mine)]
        + [(lax.rem(z + step, nz) * 2 + core, mine) for step in range(1, nz)]
        + [(z * 2 + core, y * side + lax.rem(x + step, side)) for step in range(1, side)]
        + [(z * 2 + core, lax.rem(y + step, side) * side + x) for step in range(1, side)]
    )


def remote(source, target, send_sem, recv_sem, device):
    return pltpu.make_async_remote_copy(
        src_ref=source,
        dst_ref=target,
        send_sem=send_sem,
        recv_sem=recv_sem,
        device_id=device,
        device_id_type=MESH,
    )


def loop(count, body, start=0):
    def step(index, carry):
        body(index)
        return carry

    lax.fori_loop(start, count, step, 0)


def ortho_kernel(
    ndp,
    nf,
    attn_ref,
    ffn_ref,
    attn_out,
    ffn_out,
    land_attn,
    land_ffn,
    iter_low,
    iter_full,
    gram,
    gram_send,
    gram_recv,
    off_low,
    poly_low,
    diag_row,
    diag_col,
    inverse_norm,
    own_low,
    own_full,
    own_attn,
    own_ffn,
    own_sem,
    piece_send,
    piece_recv,
    first_send,
    second_send,
    plane_recv,
    gram_send_sem,
    gram_recv_sem,
    back_send,
    back_recv,
):
    z, core, y, x, nz, side = place(ndp, nf)
    dp, fs = z * 2 + core, y * side + x
    rows = attn_ref.shape[1]
    size = rows * ndp
    is_attn = jnp.logical_or(dp < 2, jnp.logical_and(dp >= 6, dp < ROLES))
    is_ffn = jnp.logical_and(dp >= 2, dp < 6)
    partner = z * 2 + 1 - core

    greet(
        [(lax.rem(dp + step, ndp), fs) for step in range(1, ndp)]
        + [(dp, y * side + lax.rem(x + step, side)) for step in range(1, side)]
        + [(dp, lax.rem(y + step, side) * side + x) for step in range(1, side)]
    )

    def piece(role):
        if role < 2 or role >= 6:
            return attn_ref.at[role if role < 2 else role - 4], land_attn
        return ffn_ref.at[(role - 2) // 2, (role - 2) % 2], land_ffn

    def piece_copy(role):
        source, land = piece(role)
        return remote(source, land.at[fs, dp], piece_send.at[role], piece_recv.at[dp], (role, fs))

    for role in (2, 4, 3, 5, 0, 6, 1, 7):
        @pl.when(dp != role)
        def _(role=role):
            piece_copy(role).start()

        @pl.when(dp == role)
        def _(role=role):
            source, land = piece(role)
            pltpu.make_async_copy(source, land.at[fs, dp], own_sem).start()

    def along(first, step):
        x_at = jnp.where(first, lax.rem(x + step, side), x)
        y_at = jnp.where(first, y, lax.rem(y + step, side))
        return y_at * side + x_at

    def iterate(land, source, own_out, target, role, paired):
        width = land.shape[-1]
        columns = width * nf
        tall = min(STEP_ROWS, size)
        steps = size // tall
        wide = min(1024, columns)

        def row_of(index):
            return lax.rem(z + index // 2, nz) * 2 + lax.rem(core + index, 2)

        def x_first(row):
            return lax.rem(row // 2, 2) == 0

        def first_copy(row, step):
            here = land.at[fs, row]
            peer = along(x_first(row), step)
            return remote(here, here, first_send.at[row, step - 1], plane_recv.at[fs, row], (dp, peer))

        def second_copy(plane_at, row, line, step):
            here = land.at[plane_at, row]
            peer = along(jnp.logical_not(x_first(row)), step)
            return remote(
                here, here, second_send.at[row, line, step - 1], plane_recv.at[plane_at, row], (dp, peer)
            )

        def arrived(plane_at, row):
            here = land.at[plane_at, row]
            remote(here, here, own_sem, plane_recv.at[plane_at, row], (dp, fs)).wait_recv()

        def take_piece(index):
            row = row_of(index)

            @pl.when(index == 0)
            def _():
                pltpu.make_async_copy(source, land.at[fs, row], own_sem).wait()

            @pl.when(index > 0)
            def _():
                remote(source, land.at[fs, row], own_sem, piece_recv.at[row], (dp, fs)).wait_recv()

            for step in range(1, side):
                first_copy(row, step).start()
                second_copy(fs, row, 0, step).start()

        loop(ndp, take_piece)

        def pass_on(index):
            row = row_of(index)
            for line in range(1, side):
                plane_at = along(x_first(row), line)
                arrived(plane_at, row)
                for step in range(1, side):
                    second_copy(plane_at, row, line, step).start()

        def add_gram(plane_at, fresh):
            block = land[plane_at].reshape(size, width)
            for step in range(steps):
                at = slice(step * tall, (step + 1) * tall)
                part = contract_cols(block[at], block)
                if fresh:
                    gram[at] = part
                else:
                    gram[at] += part

        add_gram(fs, True)
        loop(ndp, pass_on)

        for line in range(side):
            for step in range(1, side):

                def last(index, line=line, step=step):
                    row = row_of(index)
                    near = jnp.where(
                        x_first(row),
                        lax.rem(y + step, side) * side + lax.rem(x + line, side),
                        lax.rem(y + line, side) * side + lax.rem(x + step, side),
                    )
                    arrived(near, row)

                loop(ndp, last)
            if line == 0:
                for step in range(1, side):
                    add_gram(along(True, step), False)
                    add_gram(along(False, step), False)
        for far_y in range(1, side):
            for far_x in range(1, side):
                add_gram(lax.rem(y + far_y, side) * side + lax.rem(x + far_x, side), False)

        def gram_copy(slot, step):
            at = pl.ds(step * tall, tall)
            return remote(
                gram_send.at[slot, at],
                gram_recv.at[slot, at],
                gram_send_sem.at[slot, step],
                gram_recv_sem.at[slot, step],
                (partner, fs),
            )

        if paired:
            for step in range(steps):
                at = slice(step * tall, (step + 1) * tall)
                gram_send[0, at] = gram[at].astype(jnp.bfloat16)
                gram_copy(0, step).start()
        for index in range(nf):
            block = land[index].reshape(size, width)
            at = slice(index * width, (index + 1) * width)
            iter_low[0, :, at] = block
            iter_full[:, at] = block.astype(jnp.float32)

        def back_copy(row):
            return remote(own_out.at[row], target, back_send.at[row], back_recv.at[role], (row, fs))

        def iteration(count):
            now = lax.rem(count, 2)
            later = 1 - now

            @pl.when(count > 0)
            def _():
                def gram_rows(step):
                    at = pl.ds(pl.multiple_of(step * tall, tall), tall)
                    part = contract_cols(iter_low[now, at, :columns], iter_low[now, :, :columns])
                    if paired:
                        gram_send[now, at] = part.astype(jnp.bfloat16)
                        gram_copy(now, step).start()
                    else:
                        gram[at] = part

                loop(steps, gram_rows)

            eye = lax.broadcasted_iota(jnp.int32, (TILE_ROWS, TILE_ROWS), 0) == lax.broadcasted_iota(
                jnp.int32, (TILE_ROWS, TILE_ROWS), 1
            )

            @pl.when(count == 0)
            def _():
                trace = jnp.zeros((TILE_ROWS, TILE_ROWS), jnp.float32)
                if paired:
                    for step in range(steps):
                        gram_copy(now, step).wait()
                for tile in range(size // TILE_ROWS):
                    at = slice(tile * TILE_ROWS, (tile + 1) * TILE_ROWS)
                    if paired:
                        square = gram_send[now, at, at].astype(jnp.float32)
                        trace += square + gram_recv[now, at, at].astype(jnp.float32)
                    else:
                        trace += gram[at, at]
                trace = jnp.sum(jnp.where(eye, trace, 0.0), axis=1, keepdims=True)
                trace = jnp.sum(trace, axis=0, keepdims=True)
                inverse_norm[...] = 1.0 / (jnp.sqrt(trace) + norm_epsilon)

            @pl.when(count > 0)
            def _():
                inverse_norm[...] = jnp.ones_like(inverse_norm)

            inverse = inverse_norm[...]
            shrink = inverse * inverse

            for step in range(steps):
                if paired:
                    @pl.when(count > 0)
                    def _(step=step):
                        gram_copy(now, step).wait()

                for tile in range(step * tall // TILE_ROWS, (step + 1) * tall // TILE_ROWS):
                    at = slice(tile * TILE_ROWS, (tile + 1) * TILE_ROWS)
                    if paired:
                        total = gram_send[now, at].astype(jnp.float32) + gram_recv[now, at].astype(jnp.float32)
                    else:
                        total = gram[at]
                    total = total * shrink
                    gram[at] = total
                    off_low[at] = total.astype(jnp.bfloat16)
                    square = total[:, at]
                    masked = jnp.where(eye, square, 0.0)
                    diag_col[at] = jnp.sum(masked, axis=1, keepdims=True)
                    diag_row[:, at] = jnp.sum(masked, axis=0, keepdims=True)
                    square = jnp.where(eye, 0.0, square)
                    gram[at, at] = square
                    off_low[at, at] = square.astype(jnp.bfloat16)

            linear, middle, cubic = ns_linear * inverse, ns_square * inverse, ns_cubic * inverse

            def poly_rows(step):
                at = pl.ds(step * tall, tall)
                again = product(off_low[at], off_low[...])
                mine = diag_col[at]
                poly = gram[at] * (middle + cubic * mine + cubic * diag_row[...]) + cubic * again
                poly_low[at] = poly.astype(jnp.bfloat16)
                again_diag = []
                for tile in range(tall // TILE_ROWS):
                    rows_at = slice(tile * TILE_ROWS, (tile + 1) * TILE_ROWS)
                    side_at = slice(step * tall + tile * TILE_ROWS, step * tall + (tile + 1) * TILE_ROWS)
                    again_diag.append(
                        jnp.sum(jnp.where(eye, again[rows_at, side_at], 0.0), axis=1, keepdims=True)
                    )
                    poly_low[side_at, side_at] = jnp.where(eye, 0.0, poly[rows_at, side_at]).astype(jnp.bfloat16)
                again_diag = jnp.concatenate(again_diag, axis=0)
                factor = linear + middle * mine + cubic * (mine * mine + again_diag)

                @pl.when(count < ITERS - 1)
                def _():
                    for left in range(0, columns, wide):
                        part = slice(left, left + wide)
                        moved = product(poly_low[at], iter_low[now, :, part])
                        fresh = factor * iter_full[at, part] + moved
                        iter_full[at, part] = fresh
                        iter_low[later, at, part] = fresh.astype(jnp.bfloat16)

                @pl.when(count == ITERS - 1)
                def _():
                    for index in range(nf):
                        @pl.when(fs == index)
                        def _(index=index):
                            part = slice(index * width, (index + 1) * width)
                            own_full[at, :width] = iter_full[at, part]

                            if step == 0:
                                own_low[:, :width] = iter_low[now, :, part]

                    moved = product(poly_low[at], own_low[:, :width])
                    fresh = factor * own_full[at, :width] + moved
                    blocks = tall // rows
                    own_out[pl.ds(step * blocks, blocks)] = fresh.astype(jnp.bfloat16).reshape(
                        blocks, rows, width
                    )

                    def give(index):
                        row = step * blocks + index

                        @pl.when(row != dp)
                        def _():
                            back_copy(row).start()

                        @pl.when(row == dp)
                        def _():
                            pltpu.make_async_copy(own_out.at[row], target, own_sem).start()

                    loop(blocks, give)

            for step in range(steps):
                poly_rows(step)

        loop(ITERS, iteration)

        def finish(row):
            for step in range(1, side):
                first_copy(row, step).wait_send()
                for line in range(side):
                    second_copy(fs, row, line, step).wait_send()

            @pl.when(row != dp)
            def _():
                back_copy(row).wait_send()

        loop(ndp, finish)
        pltpu.make_async_copy(own_out.at[dp], target, own_sem).wait()

    @pl.when(is_attn)
    def _():
        at = jnp.where(dp < 2, dp, dp - 4)
        iterate(land_attn, attn_ref.at[at], own_attn, attn_out.at[at], dp, False)

    @pl.when(is_ffn)
    def _():
        matrix, half = (dp - 2) // 2, lax.rem(dp - 2, 2)
        iterate(land_ffn, ffn_ref.at[matrix, half], own_ffn, ffn_out.at[matrix, half], dp, True)

    for role in range(ROLES):
        @pl.when(dp != role)
        def _(role=role):
            if role < 2 or role >= 6:
                target = attn_out.at[role if role < 2 else role - 4]
            else:
                target = ffn_out.at[(role - 2) // 2, (role - 2) % 2]
            piece_copy(role).wait_send()
            remote(target, target, own_sem, back_recv.at[role], (role, fs)).wait_recv()


def orthogonalize(ndp, nf, attn_low, ffn_low):
    rows, width_attn = attn_low.shape[1:]
    width_ffn = ffn_low.shape[3]
    side = math.isqrt(nf)
    size = rows * ndp
    columns = width_ffn * nf
    tall = min(STEP_ROWS, size)
    bf16, f32 = jnp.bfloat16, jnp.float32
    dma = pltpu.SemaphoreType.DMA
    return pl.pallas_call(
        functools.partial(ortho_kernel, ndp, nf),
        name="newton_schulz",
        out_shape=[
            jax.ShapeDtypeStruct(attn_low.shape, bf16),
            jax.ShapeDtypeStruct(ffn_low.shape, bf16),
        ],
        in_specs=[pl.BlockSpec(memory_space=pltpu.VMEM)] * 2,
        out_specs=[pl.BlockSpec(memory_space=pltpu.VMEM)] * 2,
        scratch_shapes=[
            pltpu.VMEM((nf, ndp, rows, width_attn), bf16),
            pltpu.VMEM((nf, ndp, rows, width_ffn), bf16),
            pltpu.VMEM((2, size, columns), bf16),
            pltpu.VMEM((size, columns), f32),
            pltpu.VMEM((size, size), f32),
            pltpu.VMEM((2, size, size), bf16),
            pltpu.VMEM((2, size, size), bf16),
            pltpu.VMEM((size, size), bf16),
            pltpu.VMEM((size, size), bf16),
            pltpu.VMEM((1, size), f32),
            pltpu.VMEM((size, 1), f32),
            pltpu.VMEM((1, 1), f32),
            pltpu.VMEM((size, width_ffn), bf16),
            pltpu.VMEM((size, width_ffn), f32),
            pltpu.VMEM((ndp, rows, width_attn), bf16),
            pltpu.VMEM((ndp, rows, width_ffn), bf16),
            dma,
            dma((ROLES,)),
            dma((ndp,)),
            dma((ndp, side - 1)),
            dma((ndp, side, side - 1)),
            dma((nf, ndp)),
            dma((2, size // tall)),
            dma((2, size // tall)),
            dma((ndp,)),
            dma((ROLES,)),
        ],
        compiler_params=pltpu.CompilerParams(
            collective_id=1, has_side_effects=True, vmem_limit_bytes=60 * 1024 * 1024
        ),
    )(attn_low, ffn_low)


def update_kernel(
    attn_w,
    ffn_w,
    vectors,
    attn_mom,
    ffn_mom,
    vec_mom,
    attn_ema,
    ffn_ema,
    vec_ema,
    attn_grad,
    up_grad,
    down_grad,
    vec_grad,
    attn_ortho,
    ffn_ortho,
    attn_new,
    ffn_new,
    vec_new,
    attn_mom_new,
    ffn_mom_new,
    vec_mom_new,
    attn_ema_new,
    ffn_ema_new,
    vec_ema_new,
    *,
    vector_rate,
):
    for index in range(4):
        rate = attn_rates[index]
        attn_mom_new[index] = matrix_decay * attn_mom[index] + attn_grad[index]
        new = attn_w[index] * (1.0 - weight_decay * rate) - rate * attn_ortho[index].astype(jnp.float32)
        attn_new[index] = new
        attn_ema_new[index] = average_decay * attn_ema[index] + (1.0 - average_decay) * new
    width = ffn_ortho.shape[-1]
    shape_factor = math.sqrt(FF / D)
    for index, grad in enumerate((up_grad, down_grad)):
        ffn_mom_new[index] = matrix_decay * ffn_mom[index] + grad[...]
        for half in range(2):
            at = slice(half * width, (half + 1) * width)
            ortho = ffn_ortho[index, half].astype(jnp.float32)
            new = ffn_w[index, :, at] * (1.0 - weight_decay) - shape_factor * ortho
            ffn_new[index, :, at] = new
            ffn_ema_new[index, :, at] = average_decay * ffn_ema[index, :, at] + (1.0 - average_decay) * new
    mom = vector_decay * vec_mom[...] + vec_grad[...]
    vec_mom_new[...] = mom
    new = vectors[...] - vector_rate * mom
    vec_new[...] = new
    vec_ema_new[...] = average_decay * vec_ema[...] + (1.0 - average_decay) * new


def update_all(vector_rate, *operands):
    states = operands[:9]
    return pl.pallas_call(
        functools.partial(update_kernel, vector_rate=vector_rate),
        name="update",
        out_shape=[jax.ShapeDtypeStruct(states[index % 3].shape, jnp.float32) for index in range(9)],
        in_specs=[pl.BlockSpec(memory_space=pltpu.VMEM)] * len(operands),
        out_specs=[pl.BlockSpec(memory_space=pltpu.VMEM)] * 9,
        compiler_params=pltpu.CompilerParams(vmem_limit_bytes=60 * 1024 * 1024),
    )(*operands)


ROOM = pltpu.CompilerParams(vmem_limit_bytes=56 * 1024 * 1024)
ROOT_HALF = math.sqrt(0.5)
BELL = 1.0 / math.sqrt(2.0 * math.pi)


def flat(block):
    return block.reshape(-1, block.shape[-1])


def head_lanes(values, head):
    if values.shape[1] == HDIM:
        return values
    lane = lax.broadcasted_iota(jnp.int32, values.shape, 1)
    return jnp.where(lax.div(lane, HDIM) == head, values, jnp.zeros_like(values))


def normalize(values):
    center = values - jnp.mean(values, axis=1, keepdims=True)
    inverse = lax.rsqrt(jnp.mean(center * center, axis=1, keepdims=True) + ln_epsilon)
    return center * inverse, inverse


def normalize_back(grad, scaled, inverse):
    return inverse * (
        grad
        - jnp.mean(grad, axis=1, keepdims=True)
        - scaled * jnp.mean(grad * scaled, axis=1, keepdims=True)
    )


def row_sum(values):
    return jnp.sum(values.astype(jnp.float32), axis=0, keepdims=True)


def forward_kernel(
    ndp,
    nf,
    tokens_ref,
    label_ref,
    cotangent_ref,
    attn_w,
    ffn_w,
    vectors_ref,
    attn_out,
    up_out,
    down_out,
    blocks_out,
    active_out,
    slope_out,
    vec_out,
    mixture_out,
    total_out,
    scaled_out,
    inverse_out,
    low_out,
    layer_out,
    d_second_out,
    sums_out,
    attn_shard,
    up_shard,
    down_shard,
    three_weight,
    out_weight,
    ffn_weight,
    vec_land,
    bias,
    bias_up,
    blocks,
    parts,
    active,
    slope,
    total,
    own_sem,
    own_recv,
    pair_recv,
    z_send,
    first_send,
    second_send,
    pair_send,
    load_sem,
    store_sem,
):
    chunks = 3
    shards, wholes = (attn_shard, up_shard, down_shard), (attn_out, up_out, down_out)
    z, core, y, x, nz, side = place(ndp, nf)
    dp, fs = z * 2 + core, y * side + x
    rows, width_attn = attn_w.shape[1:]
    width_ffn, share = ffn_w.shape[2], vectors_ref.shape[1]
    count = tokens_ref.shape[0]
    width = ffn_weight.shape[-1]
    per = width_ffn // width

    attn_shard[4 * rows :] = jnp.zeros((16, width_attn), jnp.bfloat16)
    attn_shard[4 * rows : 4 * rows + 12, :share] = vectors_ref[...].astype(jnp.bfloat16)
    for index in range(4):
        attn_shard[index * rows : (index + 1) * rows] = attn_w[index].astype(jnp.bfloat16)
    up_shard[...] = ffn_w[0].astype(jnp.bfloat16)
    down_shard[...] = ffn_w[1].astype(jnp.bfloat16)
    greet(line_partners(ndp, nf))

    def slot(chunk, plane_at, z_at):
        return wholes[chunk].at[plane_at, z_at * 2 + core]

    def source(chunk, plane_at, z_at, own):
        return shards[chunk] if own else slot(chunk, plane_at, z_at)

    def along(first, step):
        x_at = jnp.where(first, lax.rem(x + step, side), x)
        y_at = jnp.where(first, y, lax.rem(y + step, side))
        return y_at * side + x_at

    def first_copy(chunk, z_at, step, own):
        peer = along(lax.rem(z_at, 2) == 0, step)
        return remote(
            source(chunk, fs, z_at, own),
            slot(chunk, fs, z_at),
            first_send.at[chunk, z_at, step - 1],
            own_recv.at[chunk, fs, z_at],
            (dp, peer),
        )

    def second_copy(chunk, plane_at, z_at, step, own, line):
        peer = along(lax.rem(z_at, 2) != 0, step)
        return remote(
            source(chunk, plane_at, z_at, own),
            slot(chunk, plane_at, z_at),
            second_send.at[chunk, z_at, line, step - 1],
            own_recv.at[chunk, plane_at, z_at],
            (dp, peer),
        )

    def pair_copy(chunk, plane_at, z_at, own):
        return remote(
            source(chunk, plane_at, z_at, own),
            slot(chunk, plane_at, z_at),
            pair_send.at[chunk, plane_at, z_at],
            pair_recv.at[chunk, plane_at, z_at],
            (z * 2 + 1 - core, fs),
        )

    def z_copy(chunk, step):
        return remote(
            shards[chunk],
            slot(chunk, fs, z),
            z_send.at[chunk, step - 1],
            own_recv.at[chunk, fs, z],
            (lax.rem(z + step, nz) * 2 + core, fs),
        )

    def arrived(chunk, plane_at, z_at):
        here = slot(chunk, plane_at, z_at)
        remote(here, here, own_sem.at[chunk], own_recv.at[chunk, plane_at, z_at], (dp, fs)).wait_recv()

    def pass_on(chunk, z_at, own):
        for step in range(1, side):
            first_copy(chunk, z_at, step, own).start()
            second_copy(chunk, fs, z_at, step, own, 0).start()
        pair_copy(chunk, fs, z_at, own).start()

    def own_copy(chunk):
        return pltpu.make_async_copy(shards[chunk], slot(chunk, fs, z), own_sem.at[chunk])

    def near_first(body):
        def each(index):
            far = 1 + lax.div(index, 2)
            z_at = jnp.where(lax.rem(index, 2) == 0, z - far, z + far)

            @pl.when(jnp.logical_and(z_at >= 0, z_at < nz))
            def _():
                body(z_at)

        loop(2 * (nz - 1), each)

    def from_z(chunk):
        def each(z_at):
            arrived(chunk, fs, z_at)
            pass_on(chunk, z_at, False)

        near_first(each)

    def from_first(chunk):
        def each(z_at):
            for line in range(1, side):
                plane_at = along(lax.rem(z_at, 2) == 0, line)
                arrived(chunk, plane_at, z_at)
                for step in range(1, side):
                    second_copy(chunk, plane_at, z_at, step, False, line).start()
                pair_copy(chunk, plane_at, z_at, False).start()

        each(z)
        near_first(each)

    def last_places(z_at):
        x_first = lax.rem(z_at, 2) == 0
        for line in range(side):
            for step in range(1, side):
                near_x, far_y = lax.rem(x + line, side), lax.rem(y + step, side)
                far_x, near_y = lax.rem(x + step, side), lax.rem(y + line, side)
                yield jnp.where(x_first, far_y * side + near_x, near_y * side + far_x)

    def from_second(chunk):
        def each(z_at):
            for plane_at in last_places(z_at):
                arrived(chunk, plane_at, z_at)
                pair_copy(chunk, plane_at, z_at, False).start()

        each(z)
        near_first(each)

    def from_pair(chunk):
        own_copy(chunk).wait()

        def each(index):
            plane_at, z_at = lax.rem(index, nf), lax.div(index, nf)
            there = wholes[chunk].at[plane_at, z_at * 2 + 1 - core]
            remote(
                there, there, own_sem.at[chunk], pair_recv.at[chunk, plane_at, z_at], (dp, fs)
            ).wait_recv()

        loop(nf * nz, each)

    for chunk in range(chunks):
        own_copy(chunk).start(priority=1)
        for step in range(1, nz):
            z_copy(chunk, step).start()
        pass_on(chunk, z, True)

    from_z(0)
    from_first(0)
    from_z(1)
    from_second(0)
    from_pair(0)

    def load(index, source, target):
        return pltpu.make_async_copy(source, target, load_sem.at[index])

    def attn_load(index, block, at):
        per_block = ndp // nf
        if index == 0:
            return load(at, attn_out.at[block, :, pl.ds(0, 3 * rows)], three_weight.at[at])
        return load(
            2 + at,
            attn_out.at[:, pl.ds(block * per_block, per_block), pl.ds(3 * rows, rows)],
            out_weight.at[at],
        )

    vec_copy = load(4, attn_out.at[:, :, pl.ds(4 * rows, 16)], vec_land)
    vec_copy.start(priority=1)
    for index in range(2):
        attn_load(index, 0, 0).start(priority=1)
    vec_copy.wait()
    for row in range(ndp):
        for column in range(nf):
            left = (row * nf + column) * share
            vec_out[:, left : left + share] = vec_land[column, row, :, :share].astype(jnp.float32)
    for index in range(nf):
        at = slice(index * width_attn, (index + 1) * width_attn)
        bias[index, 0:1] = vec_out[0:1, at]
        bias[index, 1:2] = vec_out[1:2, at]
    for index in range(FF // width):
        left = index * width
        bias_up[index] = vec_out[5 + left // D : 6 + left // D, left % D : left % D + width]
    label_row = label_ref[...].astype(jnp.float32)
    label_col = jnp.transpose(jnp.broadcast_to(label_row, (128, count)))[:, 0:1]
    tokens = tokens_ref[...]
    lane = lax.broadcasted_iota(jnp.int32, (count, 128), 1)
    total[...] = jnp.broadcast_to(vec_out[2:3], (count, D))

    def attn_turn(block):
        at = lax.rem(block, 2)

        @pl.when(block < nf - 1)
        def _():
            for index in range(2):
                attn_load(index, block + 1, 1 - at).start(priority=1)

        attn_load(0, block, at).wait()
        attn_load(1, block, at).wait()
        weights = [flat(three_weight[at, :, index * rows : (index + 1) * rows]) for index in range(3)]
        queries = (product(tokens, weights[0]) + bias[block, 0:1]).astype(jnp.bfloat16)
        keys_all = product(tokens, weights[1]).astype(jnp.bfloat16)
        values_all = (product(tokens, weights[2]) + bias[block, 1:2]).astype(jnp.bfloat16)
        for index, values in enumerate((queries, keys_all, values_all)):
            blocks[block, index] = values
        pltpu.make_async_copy(blocks.at[block], blocks_out.at[block], store_sem.at[block]).start(priority=1)
        allowed = label_col == label_row
        totals = jnp.zeros((count, 128), jnp.float32)
        mixture = jnp.zeros((count, width_attn), jnp.float32)
        for head in range(width_attn // HDIM):
            scores = contract_cols(head_lanes(queries, head) * score_scale, keys_all)
            scores = jnp.where(allowed, scores, -1e30)
            top = jnp.max(scores, axis=1, keepdims=True)
            exponent = jnp.exp(scores - top)
            weight = jnp.sum(exponent, axis=1, keepdims=True)
            attention = (exponent * (1.0 / weight)).astype(jnp.bfloat16)
            totals = jnp.where(lane == head, top + jnp.log(weight), totals)
            mixture += product(attention, head_lanes(values_all, head))
        mixture = mixture.astype(jnp.bfloat16)
        parts[block] = mixture
        total_out[block] = jnp.transpose(totals)[:8]
        for index in range(nf):
            side_at = slice(index * width_attn, (index + 1) * width_attn)
            total[:, side_at] += product(mixture, flat(out_weight[at, index]))

        @pl.when(block == 0)
        def _():
            from_z(2)

        @pl.when(block == nf - 2)
        def _():
            from_first(1)

    loop(nf, attn_turn)

    def first_norm(index):
        at = pl.ds(pl.multiple_of(index * NORM_ROWS, NORM_ROWS), NORM_ROWS)
        scaled, inverse = normalize(tokens_ref[at].astype(jnp.float32) + total[at])
        scaled_out[at] = scaled
        inverse_out[at] = inverse
        normed = scaled * vec_out[3:4] + vec_out[4:5]
        low_out[at] = normed.astype(jnp.bfloat16)
        total[at] = normed + vec_out[9:10]

    loop(count // NORM_ROWS, first_norm)
    for index in range(nf):
        mixture_out[:, index * width_attn : (index + 1) * width_attn] = parts[index]

    def ffn_load(chunk, step, at):
        block, part = lax.div(step, per), lax.rem(step, per)
        left = pl.multiple_of(part * width, width)
        return load(5 + at, wholes[chunk].at[block, :, :, pl.ds(left, width)], ffn_weight.at[at])

    def ffn_steps(chunk, body, between):
        ffn_load(chunk, 0, 0).start(priority=1)

        def each(step):
            at = lax.rem(step, 2)

            @pl.when(step < FF // width - 1)
            def _():
                ffn_load(chunk, step + 1, 1 - at).start(priority=1)

            ffn_load(chunk, step, at).wait()
            body(step, at)
            between(step)

        loop(FF // width, each)

    def keep(step):
        column = pl.ds(pl.multiple_of(step * width, width), width)
        return (
            pltpu.make_async_copy(active.at[step], active_out.at[:, column], store_sem.at[nf]),
            pltpu.make_async_copy(slope.at[lax.rem(step, 2)], slope_out.at[:, column], store_sem.at[nf + 1]),
        )

    def up_step(step, at):
        up_proj = product(low_out[...], flat(ffn_weight[at])) + bias_up[step]
        half = 0.5 * (1.0 + lax.erf(up_proj * ROOT_HALF))

        @pl.when(step > 0)
        def _():
            for copy in keep(step - 1):
                copy.wait()

        active[step] = (up_proj * half).astype(jnp.bfloat16)
        slope[lax.rem(step, 2)] = (half + up_proj * (BELL * jnp.exp(-0.5 * up_proj * up_proj))).astype(
            jnp.bfloat16
        )
        for copy in keep(step):
            copy.start(priority=1)

    def down_step(step, at):
        total[...] += contract_cols(active[step], flat(ffn_weight[at]))

    def between_up(step):
        @pl.when(step == FF // width // 2)
        def _():
            from_first(2)

    from_second(1)
    from_pair(1)
    ffn_steps(1, up_step, between_up)
    for copy in keep(FF // width - 1):
        copy.wait()
    from_second(2)
    from_pair(2)
    ffn_steps(2, down_step, lambda step: None)
    sums_out[...] = jnp.zeros((8, D), jnp.float32)

    def second_norm(index):
        at = pl.ds(pl.multiple_of(index * NORM_ROWS, NORM_ROWS), NORM_ROWS)
        scaled, inverse = normalize(total[at])
        layer_out[at] = (scaled * vec_out[10:11] + vec_out[11:12]).astype(jnp.bfloat16)
        grad = cotangent_ref[at].astype(jnp.float32)
        d_second = normalize_back(grad * vec_out[10:11], scaled, inverse)
        d_second_out[at] = d_second
        sums_out[0:1] += row_sum(d_second.astype(jnp.bfloat16))
        sums_out[1:2] += row_sum(grad * scaled)
        sums_out[2:3] += row_sum(grad)

    loop(count // NORM_ROWS, second_norm)

    def stored(block):
        pltpu.make_async_copy(blocks.at[block], blocks_out.at[block], store_sem.at[block]).wait()

    loop(nf, stored)
    for chunk in range(chunks):
        for step in range(1, nz):
            z_copy(chunk, step).wait_send()

        def finish(z_at):
            for step in range(1, side):
                first_copy(chunk, z_at, step, False).wait_send()
                for line in range(side):
                    second_copy(chunk, fs, z_at, step, False, line).wait_send()

            def each(plane_at):
                pair_copy(chunk, plane_at, z_at, False).wait_send()

            loop(nf, each)

        loop(nz, finish)


def forward(ndp, nf, tokens, segments, cotangent, attn_w, ffn_w, vectors):
    nz, side, chunks = ndp // 2, math.isqrt(nf), 3
    count = tokens.shape[0]
    rows, width_attn = attn_w.shape[1:]
    width_ffn = ffn_w.shape[2]
    width = min(512, width_ffn)
    bf16, f32 = jnp.bfloat16, jnp.float32
    dma = pltpu.SemaphoreType.DMA
    anywhere, inside = pl.BlockSpec(memory_space=pl.ANY), pl.BlockSpec(memory_space=pltpu.VMEM)
    shape = jax.ShapeDtypeStruct
    return pl.pallas_call(
        functools.partial(forward_kernel, ndp, nf),
        name="forward",
        out_shape=[
            shape((nf, ndp, 4 * rows + 16, width_attn), bf16),
            shape((nf, ndp, rows, width_ffn), bf16),
            shape((nf, ndp, rows, width_ffn), bf16),
            shape((nf, 3, count, width_attn), bf16),
            shape((count, FF), bf16),
            shape((count, FF), bf16),
            shape((16, D), f32),
            shape((count, D), bf16),
            shape((nf, 8, count), f32),
            shape((count, D), f32),
            shape((count, 1), f32),
            shape((count, D), bf16),
            shape((count, D), bf16),
            shape((count, D), f32),
            shape((8, D), f32),
        ],
        in_specs=[inside] * 6,
        out_specs=[anywhere] * 6 + [inside] * 9,
        scratch_shapes=[
            pltpu.VMEM((4 * rows + 16, width_attn), bf16),
            pltpu.VMEM((rows, width_ffn), bf16),
            pltpu.VMEM((rows, width_ffn), bf16),
            pltpu.VMEM((2, ndp, 3 * rows, width_attn), bf16),
            pltpu.VMEM((2, nf, ndp // nf, rows, width_attn), bf16),
            pltpu.VMEM((2, ndp, rows, width), bf16),
            pltpu.VMEM((nf, ndp, 16, width_attn), bf16),
            pltpu.VMEM((nf, 8, width_attn), f32),
            pltpu.VMEM((FF // width, 1, width), f32),
            pltpu.VMEM((nf, 3, count, width_attn), bf16),
            pltpu.VMEM((nf, count, width_attn), bf16),
            pltpu.VMEM((FF // width, count, width), bf16),
            pltpu.VMEM((2, count, width), bf16),
            pltpu.VMEM((count, D), f32),
            dma((chunks,)),
            dma((chunks, nf, nz)),
            dma((chunks, nf, nz)),
            dma((chunks, nz - 1)),
            dma((chunks, nz, side - 1)),
            dma((chunks, nz, side, side - 1)),
            dma((chunks, nf, nz)),
            dma((7,)),
            dma((nf + 2,)),
        ],
        compiler_params=pltpu.CompilerParams(
            collective_id=2, has_side_effects=True, vmem_limit_bytes=60 * 1024 * 1024
        ),
    )(tokens, segments[None, :], cotangent, attn_w, ffn_w, vectors)


def backward_kernel(
    ndp,
    nf,
    d_second_ref,
    low_ref,
    scaled_ref,
    inverse_ref,
    vec_ref,
    active_ref,
    slope_ref,
    up_ref,
    down_ref,
    tokens_ref,
    label_ref,
    blocks_ref,
    mixture_ref,
    total_ref,
    attn_ref,
    tail_ref,
    attn_mom,
    ffn_mom,
    input_grad,
    up_out,
    down_out,
    attn_out,
    vec_out,
    attn_low,
    ffn_low,
    held_up,
    held_down,
    held_attn,
    first_up,
    first_down,
    first_attn,
    second_up,
    second_down,
    second_attn,
    z_up,
    z_down,
    z_attn,
    stages_out,
    land,
    ffn_weight,
    ffn_act,
    attn_weight,
    attn_block,
    wide_low,
    wide_two,
    turned_one,
    turned_two,
    branch,
    bias_up_sum,
    query_sum,
    value_sum,
    vec_land,
    load_sem,
    step_sem,
    pair_send,
    pair_recv,
    first_send,
    first_recv,
    second_send,
    second_recv,
    z_send,
    z_recv,
    vec_send,
    vec_recv,
):
    z, core, y, x, nz, side = place(ndp, nf)
    dp, fs = z * 2 + core, y * side + x
    other = (z * 2 + 1 - core, fs)
    held, outs = (held_up, held_down, held_attn), (up_out, down_out, attn_out)
    from_first, from_second = (first_up, first_down, first_attn), (second_up, second_down, second_attn)
    from_z = (z_up, z_down, z_attn)
    chunks = 3
    rows, width_ffn = held_up.shape[2:]
    width_attn = held_attn.shape[-1]
    width = ffn_weight.shape[-1]
    per = width_ffn // width
    greet(line_partners(ndp, nf))

    def place_of(turn):
        step = nf - 1 - turn
        return lax.rem(y + lax.div(step, side), side) * side + lax.rem(x + lax.rem(step, side), side)

    def first_copy(chunk, z_at, line, step):
        x_first = lax.rem(z_at, 2) == 0
        near, far = lax.rem(x + step, side), lax.rem(y + step, side)
        to = jnp.where(x_first, y * side + near, far * side + x)
        at = jnp.where(
            x_first,
            lax.rem(y + line, side) * side + near,
            far * side + lax.rem(x + line, side),
        )
        return remote(
            held[chunk].at[z_at, at],
            from_first[chunk].at[z_at, step - 1, line],
            first_send.at[chunk, z_at, step - 1, line],
            first_recv.at[chunk, z_at, step - 1, line],
            (dp, to),
        )

    lag = 2
    total_steps = nf * per + nf
    schedule = {}
    for sent, base, stride in (((0, 1), 0, per), ((2,), nf * per, 1)):
        for turns in ((0,), tuple(range(1, nf - 1))):
            ready = min(base + (turns[-1] + 1) * stride - 1 + lag, total_steps)
            for z_at in range(0, nz, 2):
                schedule.setdefault(ready, []).extend((chunk, turns, z_at) for chunk in sent)

    def send_first(chunk, turns, z_from):
        def each(z_at):
            x_first = lax.rem(z_at, 2) == 0
            for turn in turns:
                step_x, step_y = (nf - 1 - turn) % side, (nf - 1 - turn) // side
                step = jnp.where(x_first, step_x, step_y)
                line = jnp.where(x_first, step_y, step_x)

                @pl.when(step > 0)
                def _(line=line, step=step):
                    first_copy(chunk, z_at, line, step).start()

        loop(z_from + 2, each, z_from)

    def sends_at(step, steps):
        for when in steps:
            @pl.when(step == when)
            def _(when=when):
                for chunk, turns, z_at in schedule.get(when, ()):
                    send_first(chunk, turns, z_at)

    def line_place(z_at, line):
        x_first = lax.rem(z_at, 2) == 0
        return jnp.where(
            x_first, lax.rem(y + line, side) * side + x, y * side + lax.rem(x + line, side)
        )

    def second_copy(chunk, z_at, step):
        to = line_place(z_at, step)
        return remote(
            held[chunk].at[z_at, to],
            from_second[chunk].at[z_at, step - 1],
            second_send.at[chunk, z_at, step - 1],
            second_recv.at[chunk, z_at, step - 1],
            (dp, to),
        )

    def z_copy(chunk, step):
        z_at = lax.rem(z + step, nz)
        return remote(
            held[chunk].at[z_at, fs],
            from_z[chunk].at[step - 1],
            z_send.at[chunk, step - 1],
            z_recv.at[chunk, step - 1],
            (z_at * 2 + core, fs),
        )

    def take_first(chunk):
        def each(hop):
            z_at = lax.rem(z + 1 + hop, nz)
            for line in (*range(1, side), 0):
                at = line_place(z_at, line)
                for step in range(1, side):
                    first_copy(chunk, z_at, line, step).wait_recv()
                    held[chunk][z_at, at] += from_first[chunk][z_at, step - 1, line]
                if line:
                    second_copy(chunk, z_at, line).start()

        loop(nz, each)

    def take_second(chunk):
        def each(hop):
            z_at = lax.rem(z + 1 + hop, nz)
            for step in range(1, side):
                second_copy(chunk, z_at, step).wait_recv()
                held[chunk][z_at, fs] += from_second[chunk][z_at, step - 1]

            @pl.when(hop < nz - 1)
            def _():
                z_copy(chunk, hop + 1).start()

        loop(nz, each)

    def moments(chunk):
        source = ffn_mom.at[chunk] if chunk < 2 else attn_mom
        return pltpu.make_async_copy(source, outs[chunk], load_sem.at[3 + chunk])

    def take_z(chunk):
        total = held[chunk][z, fs].astype(jnp.float32)
        for step in range(1, nz):
            z_copy(chunk, step).wait_recv()
            total += from_z[chunk][step - 1].astype(jnp.float32)
        moments(chunk).wait()
        low = (matrix_decay * outs[chunk][...] + total).astype(jnp.bfloat16)
        outs[chunk][...] = total
        if chunk < 2:
            half = low.shape[1] // 2
            ffn_low[chunk, 0] = low[:, :half]
            ffn_low[chunk, 1] = low[:, half:]
        else:
            attn_low[...] = low

    vec_rounds = [[other]]
    vec_rounds.append([(dp, y * side + lax.rem(x + step, side)) for step in range(1, side)])
    vec_rounds.append([(dp, lax.rem(y + step, side) * side + x) for step in range(1, side)])
    vec_rounds.append([(lax.rem(z + step, nz) * 2 + core, fs) for step in range(1, nz)])
    starts = [sum(len(group) for group in vec_rounds[:index]) for index in range(4)]

    def vec_copy(index, step):
        at = starts[index] + step
        return remote(
            vec_land.at[index], vec_land.at[4 + at], vec_send.at[at], vec_recv.at[at], vec_rounds[index][step]
        )

    def vec_start(index):
        for step in range(len(vec_rounds[index])):
            vec_copy(index, step).start()

    def vec_take(index):
        total = vec_land[index]
        for step in range(len(vec_rounds[index])):
            vec_copy(index, step).wait_recv()
            total += vec_land[4 + starts[index] + step]
        if index < 3:
            vec_land[index + 1] = total
            vec_start(index + 1)
        else:
            vec_out[...] = total

    def split(values, keep, give):
        parts = values.astype(jnp.bfloat16).reshape(nz, 2, rows, values.shape[1])
        for which in range(2):
            @pl.when(core == which)
            def _(which=which):
                keep(parts[:, which])
                give(parts[:, 1 - which])

    def ffn_loads(slot, turn, part):
        block = place_of(turn)
        at = pl.ds(part * width, width)
        column = pl.ds(pl.multiple_of(block * width_ffn + part * width, width), width)
        pairs = (
            (up_ref.at[block, :, :, at], ffn_weight.at[slot, 0]),
            (down_ref.at[block, :, :, at], ffn_weight.at[slot, 1]),
            (active_ref.at[:, column], ffn_act.at[slot, 0]),
            (slope_ref.at[:, column], ffn_act.at[slot, 1]),
        )
        return [
            pltpu.make_async_copy(source, target, step_sem.at[slot, index])
            for index, (source, target) in enumerate(pairs)
        ]

    def load(index, source, target):
        return pltpu.make_async_copy(source, target, load_sem.at[index])

    load(0, low_ref, wide_low).start(priority=1)
    load(1, d_second_ref, input_grad).start(priority=1)
    for copy in ffn_loads(0, 0, 0):
        copy.start(priority=1)
    load(2, tokens_ref, wide_two).start(priority=1)
    for chunk in range(chunks):
        moments(chunk).start(priority=1)
    load(0, low_ref, wide_low).wait()
    turned_one[...] = jnp.transpose(wide_low[...])
    load(1, d_second_ref, input_grad).wait()
    wide_low[...] = input_grad[...].astype(jnp.bfloat16)
    turned_two[...] = jnp.transpose(wide_low[...])

    def pair_copy(step):
        stage, slot = lax.rem(step, lag), lax.rem(step, 2 * lag)
        return remote(stages_out.at[stage], land.at[slot], pair_send.at[stage], pair_recv.at[slot], other)

    def pair_take(step):
        pair_copy(step).wait()
        slot = lax.rem(step, 2 * lag)

        @pl.when(step < nf * per)
        def _():
            block, part = place_of(lax.div(step, per)), lax.rem(step, per)
            for index in range(2):
                for which in range(per):
                    @pl.when(part == which)
                    def _(index=index, which=which):
                        for half in range(2):
                            left = which * width + half * width_attn
                            at = slice(left, left + width_attn)
                            held[index][:, block, :, at] += land[slot, :, 2 * index + half]

        @pl.when(step >= nf * per)
        def _():
            held_attn[:, place_of(step - nf * per)] += land[slot]

    def ffn_turn(turn):
        block = place_of(turn)
        for part in range(per):
            now = turn * per + part
            slot = lax.rem(now, 2)
            if part < per - 1:
                for copy in ffn_loads(1 - slot, turn, part + 1):
                    copy.start(priority=1)
            else:
                @pl.when(turn < nf - 1)
                def _():
                    for copy in ffn_loads(1 - slot, turn + 1, 0):
                        copy.start(priority=1)

            for copy in ffn_loads(slot, turn, part):
                copy.wait()
            d_active = product(wide_low[...], flat(ffn_weight[slot, 1]))
            d_up = (d_active * ffn_act[slot, 1].astype(jnp.float32)).astype(jnp.bfloat16)
            bias_up_sum[block * per + part] = row_sum(d_up)
            input_grad[...] += contract_cols(d_up, flat(ffn_weight[slot, 0]))

            @pl.when(now >= lag)
            def _():
                pair_take(now - lag)

            sends_at(now, range(nf * per))
            at = slice(part * width, (part + 1) * width)
            for index in range(2):

                def keep(values, index=index):
                    held[index][:, block, :, at] = values

                def give(values, index=index):
                    for half in range(2):
                        side_at = slice(half * width_attn, (half + 1) * width_attn)
                        stages_out[lax.rem(now, lag), :, 2 * index + half] = values[:, :, side_at]

                if index == 0:
                    split(product(turned_one[...], d_up), keep, give)
                else:
                    split(product(turned_two[...], ffn_act[slot, 0]), keep, give)
            pair_copy(now).start()

    loop(nf, ffn_turn)

    load(2, tokens_ref, wide_two).wait()
    turned_one[...] = jnp.transpose(wide_two[...])
    load(0, mixture_ref, wide_two).start(priority=1)

    def attn_load(index, turn):
        block = place_of(turn)
        per_block = ndp // nf
        source, target = (
            (attn_ref.at[block, :, pl.ds(0, 3 * rows)], attn_weight[0]),
            (
                attn_ref.at[:, pl.ds(block * per_block, per_block), pl.ds(3 * rows, rows)],
                attn_weight[1],
            ),
            (blocks_ref.at[block], attn_block),
        )[index]
        return pltpu.make_async_copy(source, target, step_sem.at[0, index])

    for index in range(3):
        attn_load(index, 0).start(priority=1)
    vec_land[0] = jnp.zeros((16, D), jnp.float32)
    vec_land[0, 9:12] = tail_ref[0:3]

    def norm_back(index):
        at = pl.ds(pl.multiple_of(index * NORM_ROWS, NORM_ROWS), NORM_ROWS)
        grad = input_grad[at]
        scaled = scaled_ref[at]
        d_first = normalize_back(grad * vec_ref[3:4], scaled, inverse_ref[at])
        input_grad[at] = d_first
        low = d_first.astype(jnp.bfloat16)
        vec_land[0, 2:3] += row_sum(low)
        vec_land[0, 3:4] += row_sum(grad * scaled)
        vec_land[0, 4:5] += row_sum(grad)
        for column in range(nf):
            branch[column, at] = low[:, column * width_attn : (column + 1) * width_attn]

    loop(tokens_ref.shape[0] // NORM_ROWS, norm_back)
    label_row = label_ref[...].astype(jnp.float32)
    label_col = jnp.transpose(jnp.broadcast_to(label_row, (128, label_row.shape[1])))[:, 0:1]
    load(0, mixture_ref, wide_two).wait()
    turned_two[...] = jnp.transpose(wide_two[...])

    def attn_turn(turn):
        block = place_of(turn)
        now = nf * per + turn

        def load_next(index):
            @pl.when(turn < nf - 1)
            def _():
                attn_load(index, turn + 1).start(priority=1)

        for index in range(3):
            attn_load(index, turn).wait()
        count = tokens_ref.shape[0]
        zero = jnp.zeros((count, width_attn), jnp.float32)
        d_mixture = zero
        for index in range(nf):
            d_mixture += contract_cols(branch[index], flat(attn_weight[1][index]))
        load_next(1)
        d_mixture = d_mixture.astype(jnp.bfloat16)
        queries, keys_all, values_all = (attn_block[index] for index in range(3))
        allowed = label_col == label_row
        d_queries, d_keys, d_values = zero, zero, zero
        for head in range(width_attn // HDIM):
            my_queries = head_lanes(queries, head) * score_scale
            my_mixture = head_lanes(d_mixture, head)
            scores = contract_cols(keys_all, my_queries) - total_ref[block, head : head + 1, :]
            attention = jnp.where(allowed, jnp.exp(scores), 0.0)
            d_attention = contract_cols(values_all, my_mixture)
            inner = jnp.sum(d_attention * attention, axis=0, keepdims=True)
            d_scores = (attention * (d_attention - inner)).astype(jnp.bfloat16)
            d_keys += product(d_scores, my_queries)
            d_values += product(attention.astype(jnp.bfloat16), my_mixture)
            d_queries += contract_rows(d_scores, head_lanes(keys_all, head) * score_scale)
        load_next(2)
        grads = [values.astype(jnp.bfloat16) for values in (d_queries, d_keys, d_values)]
        query_sum[block] = row_sum(grads[0])
        value_sum[block] = row_sum(grads[2])
        moved = jnp.zeros((count, D), jnp.float32)
        for index in range(3):
            weight = attn_weight[0][:, index * rows : (index + 1) * rows]
            moved += contract_cols(grads[index], flat(weight))
        input_grad[...] += moved
        load_next(0)

        pair_take(now - lag)
        for index in range(4):
            turned, grad = (turned_one, grads[index]) if index < 3 else (turned_two, branch[block])

            def keep(values, index=index):
                held_attn[:, block, index] = values

            def give(values, index=index):
                stages_out[lax.rem(now, lag), :, index] = values

            split(product(turned[...], grad), keep, give)
        pair_copy(now).start()
        sends_at(now, range(nf * per, total_steps))

        @pl.when(turn == nf - 3)
        def _():
            take_first(0)
            take_first(1)

        @pl.when(turn == nf - 2)
        def _():
            take_second(0)
            take_second(1)

    loop(nf, attn_turn)
    for index in range(nf):
        at = slice(index * width_attn, (index + 1) * width_attn)
        vec_land[0, 0:1, at] = query_sum[index]
        vec_land[0, 1:2, at] = value_sum[index]
    for index in range(nf * per):
        left = index * width
        vec_land[0, 5 + left // D : 6 + left // D, left % D : left % D + width] = bias_up_sum[index]
    vec_start(0)
    for step in range(total_steps - lag, total_steps):
        pair_take(step)
    sends_at(total_steps, (total_steps,))

    vec_take(0)
    take_first(2)
    vec_take(1)
    take_z(0)
    take_second(2)
    vec_take(2)
    take_z(1)
    vec_take(3)
    take_z(2)

    for chunk in range(chunks):

        def finish(z_at):
            for step in range(1, side):
                second_copy(chunk, z_at, step).wait_send()
                for line in range(side):
                    first_copy(chunk, z_at, line, step).wait_send()

        loop(nz, finish)
        for step in range(1, nz):
            z_copy(chunk, step).wait_send()
    for index in range(4):
        for step in range(len(vec_rounds[index])):
            vec_copy(index, step).wait_send()


def backward_kernel_entry(ndp, nf, *refs):
    at = 18 + 7 + 12 + 2 + 2
    backward_kernel(ndp, nf, *refs[:at], refs[at : at + 2], *refs[at + 2 :])


def backward(
    ndp, nf, d_second, low, scaled, inverse, vectors, active, slope, up_all, down_all,
    tokens, segments, blocks, mixture, totals, attn_all, tail_sums, attn_mom, ffn_mom,
):
    nz, side = ndp // 2, math.isqrt(nf)
    count = tokens.shape[0]
    rows, width_ffn = up_all.shape[2:]
    width_attn = attn_all.shape[-1]
    width = 2 * width_attn
    bf16, f32 = jnp.bfloat16, jnp.float32
    dma = pltpu.SemaphoreType.DMA
    anywhere, inside = pl.BlockSpec(memory_space=pl.ANY), pl.BlockSpec(memory_space=pltpu.VMEM)
    shapes = [(rows, width_ffn), (rows, width_ffn), (4, rows, width_attn)]
    vec_copies = 1 + 2 * (side - 1) + nz - 1
    sums = []
    for lead in ((nz, nf), (nz, side - 1, side), (nz, side - 1), (nz - 1,)):
        sums += [pltpu.VMEM(lead + shape, bf16) for shape in shapes]
    return pl.pallas_call(
        functools.partial(backward_kernel_entry, ndp, nf),
        name="backward",
        out_shape=[jax.ShapeDtypeStruct((count, D), f32)]
        + [jax.ShapeDtypeStruct(shape, f32) for shape in shapes]
        + [
            jax.ShapeDtypeStruct((16, D), f32),
            jax.ShapeDtypeStruct(attn_mom.shape, bf16),
            jax.ShapeDtypeStruct((2, 2, rows, width_ffn // 2), bf16),
        ],
        in_specs=[
            anywhere,
            anywhere,
            inside,
            inside,
            inside,
            anywhere,
            anywhere,
            anywhere,
            anywhere,
            anywhere,
            inside,
            anywhere,
            anywhere,
            inside,
            anywhere,
            inside,
            anywhere,
            anywhere,
        ],
        out_specs=[inside] * 7,
        scratch_shapes=sums
        + [
            pltpu.VMEM((2, nz, 4, rows, width_attn), bf16),
            pltpu.VMEM((4, nz, 4, rows, width_attn), bf16),
            pltpu.VMEM((2, 2, ndp, rows, width), bf16),
            pltpu.VMEM((2, 2, count, width), bf16),
            pltpu.VMEM((ndp, 3 * rows, width_attn), bf16),
            pltpu.VMEM((nf, ndp // nf, rows, width_attn), bf16),
            pltpu.VMEM((3, count, width_attn), bf16),
            pltpu.VMEM((count, D), bf16),
            pltpu.VMEM((count, D), bf16),
            pltpu.VMEM((D, count), bf16),
            pltpu.VMEM((D, count), bf16),
            pltpu.VMEM((nf, count, width_attn), bf16),
            pltpu.VMEM((FF // width, 1, width), f32),
            pltpu.VMEM((nf, 1, width_attn), f32),
            pltpu.VMEM((nf, 1, width_attn), f32),
            pltpu.VMEM((4 + vec_copies, 16, D), f32),
            dma((6,)),
            dma((2, 4)),
            dma((2,)),
            dma((4,)),
            dma((3, nz, side - 1, side)),
            dma((3, nz, side - 1, side)),
            dma((3, nz, side - 1)),
            dma((3, nz, side - 1)),
            dma((3, nz - 1)),
            dma((3, nz - 1)),
            dma((vec_copies,)),
            dma((vec_copies,)),
        ],
        compiler_params=pltpu.CompilerParams(
            collective_id=3, has_side_effects=True, vmem_limit_bytes=63 * 1024 * 1024
        ),
    )(
        d_second, low, scaled, inverse, vectors, active, slope, up_all, down_all,
        tokens, segments[None, :], blocks, mixture, totals, attn_all, tail_sums, attn_mom, ffn_mom,
    )


def on_device(
    tokens,
    segments,
    cotangent,
    attn_w,
    ffn_w,
    vectors,
    attn_mom,
    ffn_mom,
    vec_mom,
    attn_ema,
    ffn_ema,
    vec_ema,
):
    ndp, nf = lax.axis_size("dp"), lax.axis_size("fsdp")
    share = vectors.shape[1]
    (
        attn_all, up_all, down_all, blocks, active, slope, vec_full, mixture, totals, scaled, inverse, low,
        layer_out, d_second, tail_sums,
    ) = forward(ndp, nf, tokens, segments, cotangent, attn_w, ffn_w, vectors)
    input_grad, up_grad, down_grad, attn_grad, vec_sum, attn_piece, ffn_piece = backward(
        ndp, nf, d_second, low, scaled, inverse, vec_full, active, slope, up_all, down_all,
        tokens, segments, blocks, mixture, totals, attn_all, tail_sums, attn_mom, ffn_mom,
    )
    mine = (lax.axis_index("dp") * nf + lax.axis_index("fsdp")) * share
    vec_grad = lax.dynamic_slice(vec_sum, (0, mine), (12, share))
    attn_ortho, ffn_ortho = orthogonalize(ndp, nf, attn_piece, ffn_piece)
    total_tokens = tokens.shape[0] * ndp * nf
    updated = update_all(
        vector_step / math.sqrt(total_tokens),
        attn_w,
        ffn_w,
        vectors,
        attn_mom,
        ffn_mom,
        vec_mom,
        attn_ema,
        ffn_ema,
        vec_ema,
        attn_grad,
        up_grad,
        down_grad,
        vec_grad,
        attn_ortho,
        ffn_ortho,
    )
    return (layer_out, input_grad, *updated, vec_grad[2])


def solution(mesh):
    in_specs = (
        P(("dp", "fsdp"), None),
        P(("dp", "fsdp")),
        P(("dp", "fsdp"), None),
        P(None, "dp", "fsdp"),
        P(None, "dp", "fsdp"),
        P(None, ("dp", "fsdp")),
        P(None, "dp", "fsdp"),
        P(None, "dp", "fsdp"),
        P(None, ("dp", "fsdp")),
        P(None, "dp", "fsdp"),
        P(None, "dp", "fsdp"),
        P(None, ("dp", "fsdp")),
    )
    out_specs = (
        P(("dp", "fsdp"), None),
        P(("dp", "fsdp"), None),
        P(None, "dp", "fsdp"),
        P(None, "dp", "fsdp"),
        P(None, ("dp", "fsdp")),
        P(None, "dp", "fsdp"),
        P(None, "dp", "fsdp"),
        P(None, ("dp", "fsdp")),
        P(None, "dp", "fsdp"),
        P(None, "dp", "fsdp"),
        P(None, ("dp", "fsdp")),
        P(("dp", "fsdp")),
    )
    return jax.shard_map(
        on_device, mesh=mesh, in_specs=in_specs, out_specs=out_specs, check_vma=False
    )
```

profile of v0, /device:TPU:25, one launch (start us, length us, event | category | flops | bytes accessed | tf_op | source)
XLA Modules:
  0.0 440.1 jit_solution(13262226084196419726)
XLA Ops:
  0.6 144.4 %forward.1 = (bf16[4,8,528,256]{3,2,1,0:T(8,128)(2,1)}, bf16[4,8,128,1024]{3,2,1,0:T(8,128)(2,1)}, bf16[4,8,128,1024]{3,2,1,0:T(8,128)(2,1)}, bf16[4,3,512,256]{...) custom-call(bf16[512,1024]{1,0:T(8,128)(2,1)} %refs_9_.1, ...), custom_call_target="tpu_custom_call" | custom-call | tf_op jit(solution)/shard_map/forward/pallas_call | solution.py:998
  145.1 155.9 %backward.1 = (f32[512,1024]{1,0:T(8,128)}, f32[128,1024]{1,0:T(8,128)}, f32[128,1024]{1,0:T(8,128)}, f32[4,128,256]{2,1,0:T(8,128)}, f32[16,1024]{1,0:T(8,128)}...) custom-call(f32[512,1024]{1,0:T(8,128)} %get-tuple-element.46.refs_0_, ...), custom_call_target="tpu_custom_call" | custom-call | tf_op jit(solution)/shard_map/backward/pallas_call | solution.py:1558
  300.9 0.0 copy-start.1
  301.0 1.5 constant_dynamic-slice_fusion.vec_grad
  302.4 128.2 %newton_schulz.1 = (bf16[4,128,256]{2,1,0:T(8,128)(2,1)}, bf16[2,2,128,512]{3,2,1,0:T(8,128)(2,1)}) custom-call(bf16[4,128,256]{2,1,0:T(8,128)(2,1)} %get-tuple-element.65.attn_ref, bf16[2,2,128,512]{3,2,1,0:T(8,128)(2,1)} %get-tuple-element.66.ffn_ref), custom_call_target="tpu_custom_call" | custom-call | tf_op jit(solution)/shard_map/newton_schulz/pallas_call | solution.py:458
  430.7 0.0 copy-start
  430.7 5.6 %update.1 = (f32[4,128,256]{2,1,0:T(8,128)}, f32[2,128,1024]{2,1,0:T(8,128)}, f32[12,32]{1,0:T(8,128)}, f32[4,128,256]{2,1,0:T(8,128)}, f32[2,128,1024]{2,1,0:T(...) custom-call(f32[4,128,256]{2,1,0:T(8,128)} %attn_w.3, ...), custom_call_target="tpu_custom_call" | custom-call | tf_op jit(solution)/shard_map/update/pallas_call | solution.py:554
  436.3 1.3 dynamic-slice_bitcast_fusion
  437.6 0.0 copy-done.1
  437.6 1.0 copy.26
  438.6 0.0 copy-done
  438.6 1.3 copy.27
Async XLA Ops:
  300.9 136.6 %copy-start.1 = (bf16[512,1024]{1,0:T(8,128)(2,1)S(1)}, bf16[512,1024]{1,0:T(8,128)(2,1)}, u32[]{:S(2)}) copy-start(bf16[512,1024]{1,0:T(8,128)(2,1)} %get-tuple-element.90) | copy-start | bytes 3145732
  430.7 7.9 %copy-start = (f32[512,1024]{1,0:T(8,128)S(1)}, f32[512,1024]{1,0:T(8,128)}, u32[]{:S(2)}) copy-start(f32[512,1024]{1,0:T(8,128)} %get-tuple-element.91) | copy-start | bytes 6291460
where the time goes:
time: 447 us; the launch traced here: 440 us
  Pallas kernels  434 us (97%)
  local copies, waits for them, and re-layouts  5.02 us (1%)
    pallas_call x1, Pallas kernels, backward(): pl.pallas_call(functools.partial(backward_kernel_entry, ndp, nf), name='b...  156 us
    pallas_call x1, Pallas kernels, forward(): pl.pallas_call(functools.partial(forward_kernel, ndp, nf), name='forward'...  144 us
    pallas_call x1, Pallas kernels, orthogonalize(): pl.pallas_call(functools.partial(ortho_kernel, ndp, nf), name='newton_sch...  128 us

commit v1 on v0

--- a/solution.py
+++ b/solution.py
@@ -701,14 +701,23 @@
             (z * 2 + 1 - core, fs),
         )
 
-    def z_copy(chunk, step):
+    def z_copy(chunk, z_at, up, own):
         return remote(
-            shards[chunk],
-            slot(chunk, fs, z),
-            z_send.at[chunk, step - 1],
-            own_recv.at[chunk, fs, z],
-            (lax.rem(z + step, nz) * 2 + core, fs),
+            source(chunk, fs, z_at, own),
+            slot(chunk, fs, z_at),
+            z_send.at[chunk, z_at, up],
+            own_recv.at[chunk, fs, z_at],
+            ((z + (1 if up else -1)) * 2 + core, fs),
         )
+
+    def along_z(chunk, z_at, own, act):
+        @pl.when(jnp.logical_and(z_at <= z, z < nz - 1))
+        def _():
+            act(z_copy(chunk, z_at, 1, own))
+
+        @pl.when(jnp.logical_and(z_at >= z, z > 0))
+        def _():
+            act(z_copy(chunk, z_at, 0, own))
 
     def arrived(chunk, plane_at, z_at):
         here = slot(chunk, plane_at, z_at)
@@ -737,6 +746,7 @@
     def from_z(chunk):
         def each(z_at):
             arrived(chunk, fs, z_at)
+            along_z(chunk, z_at, False, lambda copy: copy.start())
             pass_on(chunk, z_at, False)
 
         near_first(each)
@@ -784,8 +794,7 @@
 
     for chunk in range(chunks):
         own_copy(chunk).start(priority=1)
-        for step in range(1, nz):
-            z_copy(chunk, step).start()
+        along_z(chunk, z, True, lambda copy: copy.start())
         pass_on(chunk, z, True)
 
     from_z(0)
@@ -968,10 +977,8 @@
 
     loop(nf, stored)
     for chunk in range(chunks):
-        for step in range(1, nz):
-            z_copy(chunk, step).wait_send()
-
         def finish(z_at):
+            along_z(chunk, z_at, False, lambda copy: copy.wait_send())
             for step in range(1, side):
                 first_copy(chunk, z_at, step, False).wait_send()
                 for line in range(side):
@@ -1035,7 +1042,7 @@
             dma((chunks,)),
             dma((chunks, nf, nz)),
             dma((chunks, nf, nz)),
-            dma((chunks, nz - 1)),
+            dma((chunks, nz, 2)),
             dma((chunks, nz, side - 1)),
             dma((chunks, nz, side, side - 1)),
             dma((chunks, nf, nz)),
@@ -1206,10 +1213,10 @@
             (z_at * 2 + core, fs),
         )
 
-    def take_first(chunk):
+    def take_first(chunk, lines):
         def each(hop):
             z_at = lax.rem(z + 1 + hop, nz)
-            for line in (*range(1, side), 0):
+            for line in lines:
                 at = line_place(z_at, line)
                 for step in range(1, side):
                     first_copy(chunk, z_at, line, step).wait_recv()
@@ -1484,10 +1491,15 @@
         pair_copy(now).start()
         sends_at(now, range(nf * per, total_steps))
 
+        @pl.when(turn == nf - 4)
+        def _():
+            take_first(0, range(1, side))
+            take_first(1, range(1, side))
+
         @pl.when(turn == nf - 3)
         def _():
-            take_first(0)
-            take_first(1)
+            take_first(0, (0,))
+            take_first(1, (0,))
 
         @pl.when(turn == nf - 2)
         def _():
@@ -1508,7 +1520,8 @@
     sends_at(total_steps, (total_steps,))
 
     vec_take(0)
-    take_first(2)
+    take_first(2, range(1, side))
+    take_first(2, (0,))
     vec_take(1)
     take_z(0)
     take_second(2)

time: 447 us -> 434 us (0.971)
  Pallas kernels: 434 us -> 422 us
    pallas_call x1, Pallas kernels: 144 us -> 139 us  [forward(): pl.pallas_call(functools.partial(forward_kernel, ndp, nf), name='forward'...]
    pallas_call x1, Pallas kernels: 156 us -> 150 us  [backward(): pl.pallas_call(functools.partial(backward_kernel_entry, ndp, nf), name='b...]
where the time goes in v1:
time: 434 us; the launch traced here: 427 us
  Pallas kernels  422 us (97%)
  local copies, waits for them, and re-layouts  5.02 us (1%)
    pallas_call x1, Pallas kernels, backward(): pl.pallas_call(functools.partial(backward_kernel_entry, ndp, nf), name='b...  150 us
    pallas_call x1, Pallas kernels, forward(): pl.pallas_call(functools.partial(forward_kernel, ndp, nf), name='forward'...  139 us
    pallas_call x1, Pallas kernels, orthogonalize(): pl.pallas_call(functools.partial(ortho_kernel, ndp, nf), name='newton_sch...  127 us

profile of v1, /device:TPU:25, one launch (start us, length us, event | category | flops | bytes accessed | tf_op | source)
XLA Modules:
  0.0 427.5 jit_solution(492701198392574356)
XLA Ops:
  0.6 138.6 %forward.1 = (bf16[4,8,528,256]{3,2,1,0:T(8,128)(2,1)}, bf16[4,8,128,1024]{3,2,1,0:T(8,128)(2,1)}, bf16[4,8,128,1024]{3,2,1,0:T(8,128)(2,1)}, bf16[4,3,512,256]{...) custom-call(bf16[512,1024]{1,0:T(8,128)(2,1)} %refs_9_.1, ...), custom_call_target="tpu_custom_call" | custom-call | tf_op jit(solution)/shard_map/forward/pallas_call | solution.py:1005
  139.3 150.1 %backward.1 = (f32[512,1024]{1,0:T(8,128)}, f32[128,1024]{1,0:T(8,128)}, f32[128,1024]{1,0:T(8,128)}, f32[4,128,256]{2,1,0:T(8,128)}, f32[16,1024]{1,0:T(8,128)}...) custom-call(f32[512,1024]{1,0:T(8,128)} %get-tuple-element.46.refs_0_, ...), custom_call_target="tpu_custom_call" | custom-call | tf_op jit(solution)/shard_map/backward/pallas_call | solution.py:1571
  289.3 0.0 copy-start.1
  289.3 1.5 constant_dynamic-slice_fusion.vec_grad
  290.8 127.2 %newton_schulz.1 = (bf16[4,128,256]{2,1,0:T(8,128)(2,1)}, bf16[2,2,128,512]{3,2,1,0:T(8,128)(2,1)}) custom-call(bf16[4,128,256]{2,1,0:T(8,128)(2,1)} %get-tuple-element.65.attn_ref, bf16[2,2,128,512]{3,2,1,0:T(8,128)(2,1)} %get-tuple-element.66.ffn_ref), custom_call_target="tpu_custom_call" | custom-call | tf_op jit(solution)/shard_map/newton_schulz/pallas_call | solution.py:458
  418.0 0.0 copy-start
  418.0 5.6 %update.1 = (f32[4,128,256]{2,1,0:T(8,128)}, f32[2,128,1024]{2,1,0:T(8,128)}, f32[12,32]{1,0:T(8,128)}, f32[4,128,256]{2,1,0:T(8,128)}, f32[2,128,1024]{2,1,0:T(...) custom-call(f32[4,128,256]{2,1,0:T(8,128)} %attn_w.3, ...), custom_call_target="tpu_custom_call" | custom-call | tf_op jit(solution)/shard_map/update/pallas_call | solution.py:554
  423.7 1.3 dynamic-slice_bitcast_fusion
  424.9 0.0 copy-done.1
  424.9 1.0 copy.26
  425.9 0.0 copy-done
  425.9 1.3 copy.27
Async XLA Ops:
  289.3 135.6 %copy-start.1 = (bf16[512,1024]{1,0:T(8,128)(2,1)S(1)}, bf16[512,1024]{1,0:T(8,128)(2,1)}, u32[]{:S(2)}) copy-start(bf16[512,1024]{1,0:T(8,128)(2,1)} %get-tuple-element.90) | copy-start | bytes 3145732
  418.0 7.9 %copy-start = (f32[512,1024]{1,0:T(8,128)S(1)}, f32[512,1024]{1,0:T(8,128)}, u32[]{:S(2)}) copy-start(f32[512,1024]{1,0:T(8,128)} %get-tuple-element.91) | copy-start | bytes 6291460

commit v2 on v1

--- a/solution.py
+++ b/solution.py
@@ -77,6 +77,16 @@
     )
 
 
+def all_partners(ndp, nf):
+    z, core, y, x, nz, side = place(ndp, nf)
+    dp, fs = z * 2 + core, y * side + x
+    return (
+        [(lax.rem(dp + step, ndp), fs) for step in range(1, ndp)]
+        + [(dp, y * side + lax.rem(x + step, side)) for step in range(1, side)]
+        + [(dp, lax.rem(y + step, side) * side + x) for step in range(1, side)]
+    )
+
+
 def remote(source, target, send_sem, recv_sem, device):
     return pltpu.make_async_remote_copy(
         src_ref=source,
@@ -96,11 +106,107 @@
     lax.fori_loop(start, count, step, 0)
 
 
+class Crossing:
+    def __init__(self, ndp, nf, land, own_sem, piece_recv, first_send, second_send, plane_recv, source):
+        self.ndp, self.land, self.own_sem, self.piece_recv, self.source = ndp, land, own_sem, piece_recv, source
+        self.first_send, self.second_send, self.plane_recv = first_send, second_send, plane_recv
+        self.z, self.core, self.y, self.x, self.nz, self.side = place(ndp, nf)
+        self.dp, self.fs = self.z * 2 + self.core, self.y * self.side + self.x
+
+    def row_of(self, index):
+        return lax.rem(self.z + index // 2, self.nz) * 2 + lax.rem(self.core + index, 2)
+
+    def x_first(self, row):
+        return lax.rem(row // 2, 2) == 0
+
+    def along(self, first, step):
+        x_at = jnp.where(first, lax.rem(self.x + step, self.side), self.x)
+        y_at = jnp.where(first, self.y, lax.rem(self.y + step, self.side))
+        return y_at * self.side + x_at
+
+    def first_copy(self, row, step):
+        here = self.land.at[self.fs, row]
+        peer = self.along(self.x_first(row), step)
+        sems = self.first_send.at[row, step - 1], self.plane_recv.at[self.fs, row]
+        return remote(here, here, *sems, (self.dp, peer))
+
+    def second_copy(self, plane_at, row, line, step):
+        here = self.land.at[plane_at, row]
+        peer = self.along(jnp.logical_not(self.x_first(row)), step)
+        sems = self.second_send.at[row, line, step - 1], self.plane_recv.at[plane_at, row]
+        return remote(here, here, *sems, (self.dp, peer))
+
+    def arrived(self, plane_at, row):
+        here = self.land.at[plane_at, row]
+        remote(here, here, self.own_sem, self.plane_recv.at[plane_at, row], (self.dp, self.fs)).wait_recv()
+
+    def take(self):
+        def each(index):
+            row = self.row_of(index)
+
+            @pl.when(index == 0)
+            def _():
+                pltpu.make_async_copy(self.source, self.land.at[self.fs, row], self.own_sem).wait()
+
+            @pl.when(index > 0)
+            def _():
+                here = self.land.at[self.fs, row]
+                remote(self.source, here, self.own_sem, self.piece_recv.at[row], (self.dp, self.fs)).wait_recv()
+
+            for step in range(1, self.side):
+                self.first_copy(row, step).start()
+                self.second_copy(self.fs, row, 0, step).start()
+
+        loop(self.ndp, each)
+
+    def pass_on(self):
+        def each(index):
+            row = self.row_of(index)
+            for line in range(1, self.side):
+                plane_at = self.along(self.x_first(row), line)
+                self.arrived(plane_at, row)
+                for step in range(1, self.side):
+                    self.second_copy(plane_at, row, line, step).start()
+
+        loop(self.ndp, each)
+
+    def wait_line(self, line):
+        for step in range(1, self.side):
+
+            def each(index, step=step):
+                row = self.row_of(index)
+                x, y, side = self.x, self.y, self.side
+                there = jnp.where(
+                    self.x_first(row),
+                    lax.rem(y + step, side) * side + lax.rem(x + line, side),
+                    lax.rem(y + line, side) * side + lax.rem(x + step, side),
+                )
+                self.arrived(there, row)
+
+            loop(self.ndp, each)
+
+    def near(self):
+        self.wait_line(0)
+
+    def far(self):
+        for line in range(1, self.side):
+            self.wait_line(line)
+
+    def finish(self):
+        def each(row):
+            for step in range(1, self.side):
+                self.first_copy(row, step).wait_send()
+                for line in range(self.side):
+                    self.second_copy(self.fs, row, line, step).wait_send()
+
+        loop(self.ndp, each)
+
+
 def ortho_kernel(
     ndp,
     nf,
     attn_ref,
-    ffn_ref,
+    ffn_whole,
     attn_out,
     ffn_out,
     land_attn,
@@ -129,6 +235,7 @@
     gram_recv_sem,
     back_send,
     back_recv,
+    load_sem,
 ):
     z, core, y, x, nz, side = place(ndp, nf)
     dp, fs = z * 2 + core, y * side + x
@@ -138,35 +245,23 @@
     is_ffn = jnp.logical_and(dp >= 2, dp < 6)
     partner = z * 2 + 1 - core
 
-    greet(
-        [(lax.rem(dp + step, ndp), fs) for step in range(1, ndp)]
-        + [(dp, y * side + lax.rem(x + step, side)) for step in range(1, side)]
-        + [(dp, lax.rem(y + step, side) * side + x) for step in range(1, side)]
-    )
+    greet(all_partners(ndp, nf))
+    attn_roles = (0, 6, 1, 7)
 
     def piece(role):
-        if role < 2 or role >= 6:
-            return attn_ref.at[role if role < 2 else role - 4], land_attn
-        return ffn_ref.at[(role - 2) // 2, (role - 2) % 2], land_ffn
+        return attn_ref.at[role if role < 2 else role - 4]
 
     def piece_copy(role):
-        source, land = piece(role)
-        return remote(source, land.at[fs, dp], piece_send.at[role], piece_recv.at[dp], (role, fs))
-
-    for role in (2, 4, 3, 5, 0, 6, 1, 7):
+        return remote(piece(role), land_attn.at[fs, dp], piece_send.at[role], piece_recv.at[dp], (role, fs))
+
+    for role in attn_roles:
         @pl.when(dp != role)
         def _(role=role):
             piece_copy(role).start()
 
         @pl.when(dp == role)
         def _(role=role):
-            source, land = piece(role)
-            pltpu.make_async_copy(source, land.at[fs, dp], own_sem).start()
-
-    def along(first, step):
-        x_at = jnp.where(first, lax.rem(x + step, side), x)
-        y_at = jnp.where(first, y, lax.rem(y + step, side))
-        return y_at * side + x_at
+            pltpu.make_async_copy(piece(role), land_attn.at[fs, dp], own_sem).start()
 
     def iterate(land, source, own_out, target, role, paired):
         width = land.shape[-1]
@@ -174,53 +269,6 @@
         tall = min(STEP_ROWS, size)
         steps = size // tall
         wide = min(1024, columns)
-
-        def row_of(index):
-            return lax.rem(z + index // 2, nz) * 2 + lax.rem(core + index, 2)
-
-        def x_first(row):
-            return lax.rem(row // 2, 2) == 0
-
-        def first_copy(row, step):
-            here = land.at[fs, row]
-            peer = along(x_first(row), step)
-            return remote(here, here, first_send.at[row, step - 1], plane_recv.at[fs, row], (dp, peer))
-
-        def second_copy(plane_at, row, line, step):
-            here = land.at[plane_at, row]
-            peer = along(jnp.logical_not(x_first(row)), step)
-            return remote(
-                here, here, second_send.at[row, line, step - 1], plane_recv.at[plane_at, row], (dp, peer)
-            )
-
-        def arrived(plane_at, row):
-            here = land.at[plane_at, row]
-            remote(here, here, own_sem, plane_recv.at[plane_at, row], (dp, fs)).wait_recv()
-
-        def take_piece(index):
-            row = row_of(index)
-
-            @pl.when(index == 0)
-            def _():
-                pltpu.make_async_copy(source, land.at[fs, row], own_sem).wait()
-
-            @pl.when(index > 0)
-            def _():
-                remote(source, land.at[fs, row], own_sem, piece_recv.at[row], (dp, fs)).wait_recv()
-
-            for step in range(1, side):
-                first_copy(row, step).start()
-                second_copy(fs, row, 0, step).start()
-
-        loop(ndp, take_piece)
-
-        def pass_on(index):
-            row = row_of(index)
-            for line in range(1, side):
-                plane_at = along(x_first(row), line)
-                arrived(plane_at, row)
-                for step in range(1, side):
-                    second_copy(plane_at, row, line, step).start()
 
         def add_gram(plane_at, fresh):
             block = land[plane_at].reshape(size, width)
@@ -232,29 +280,29 @@
                 else:
                     gram[at] += part
 
-        add_gram(fs, True)
-        loop(ndp, pass_on)
-
-        for line in range(side):
+        if paired:
+
+            def block_load(index):
+                return pltpu.make_async_copy(ffn_whole.at[index], land.at[index], load_sem.at[index])
+
+            for index in range(nf):
+                block_load(index).start()
+            for index in range(nf):
+                block_load(index).wait()
+                add_gram(index, index == 0)
+        else:
+            crossing = Crossing(ndp, nf, land, own_sem, piece_recv, first_send, second_send, plane_recv, source)
+            crossing.take()
+            add_gram(fs, True)
+            crossing.pass_on()
+            crossing.near()
             for step in range(1, side):
-
-                def last(index, line=line, step=step):
-                    row = row_of(index)
-                    near = jnp.where(
-                        x_first(row),
-                        lax.rem(y + step, side) * side + lax.rem(x + line, side),
-                        lax.rem(y + line, side) * side + lax.rem(x + step, side),
-                    )
-                    arrived(near, row)
-
-                loop(ndp, last)
-            if line == 0:
-                for step in range(1, side):
-                    add_gram(along(True, step), False)
-                    add_gram(along(False, step), False)
-        for far_y in range(1, side):
-            for far_x in range(1, side):
-                add_gram(lax.rem(y + far_y, side) * side + lax.rem(x + far_x, side), False)
+                add_gram(crossing.along(True, step), False)
+                add_gram(crossing.along(False, step), False)
+            crossing.far()
+            for far_y in range(1, side):
+                for far_x in range(1, side):
+                    add_gram(lax.rem(y + far_y, side) * side + lax.rem(x + far_x, side), False)
 
         def gram_copy(slot, step):
             at = pl.ds(step * tall, tall)
@@ -412,12 +460,10 @@
 
         loop(ITERS, iteration)
 
+        if not paired:
+            crossing.finish()
+
         def finish(row):
-            for step in range(1, side):
-                first_copy(row, step).wait_send()
-                for line in range(side):
-                    second_copy(fs, row, line, step).wait_send()
-
             @pl.when(row != dp)
             def _():
                 back_copy(row).wait_send()
@@ -433,7 +479,7 @@
     @pl.when(is_ffn)
     def _():
         matrix, half = (dp - 2) // 2, lax.rem(dp - 2, 2)
-        iterate(land_ffn, ffn_ref.at[matrix, half], own_ffn, ffn_out.at[matrix, half], dp, True)
+        iterate(land_ffn, None, own_ffn, ffn_out.at[matrix, half], dp, True)
 
     for role in range(ROLES):
         @pl.when(dp != role)
@@ -442,13 +488,14 @@
                 target = attn_out.at[role if role < 2 else role - 4]
             else:
                 target = ffn_out.at[(role - 2) // 2, (role - 2) % 2]
-            piece_copy(role).wait_send()
+            if role in attn_roles:
+                piece_copy(role).wait_send()
             remote(target, target, own_sem, back_recv.at[role], (role, fs)).wait_recv()
 
 
-def orthogonalize(ndp, nf, attn_low, ffn_low):
+def orthogonalize(ndp, nf, attn_low, ffn_whole):
     rows, width_attn = attn_low.shape[1:]
-    width_ffn = ffn_low.shape[3]
+    width_ffn = ffn_whole.shape[3]
     side = math.isqrt(nf)
     size = rows * ndp
     columns = width_ffn * nf
@@ -460,9 +507,9 @@
         name="newton_schulz",
         out_shape=[
             jax.ShapeDtypeStruct(attn_low.shape, bf16),
-            jax.ShapeDtypeStruct(ffn_low.shape, bf16),
+            jax.ShapeDtypeStruct((2, 2, rows, width_ffn), bf16),
         ],
-        in_specs=[pl.BlockSpec(memory_space=pltpu.VMEM)] * 2,
+        in_specs=[pl.BlockSpec(memory_space=pltpu.VMEM), pl.BlockSpec(memory_space=pl.ANY)],
         out_specs=[pl.BlockSpec(memory_space=pltpu.VMEM)] * 2,
         scratch_shapes=[
             pltpu.VMEM((nf, ndp, rows, width_attn), bf16),
@@ -491,11 +538,12 @@
             dma((2, size // tall)),
             dma((ndp,)),
             dma((ROLES,)),
+            dma((nf,)),
         ],
         compiler_params=pltpu.CompilerParams(
             collective_id=1, has_side_effects=True, vmem_limit_bytes=60 * 1024 * 1024
         ),
-    )(attn_low, ffn_low)
+    )(attn_low, ffn_whole)
 
 
 def update_kernel(
@@ -1083,6 +1131,7 @@
     vec_out,
     attn_low,
     ffn_low,
+    ffn_whole,
     held_up,
     held_down,
     held_attn,
@@ -1122,6 +1171,12 @@
     z_recv,
     vec_send,
     vec_recv,
+    piece_own,
+    piece_send,
+    piece_recv,
+    piece_first,
+    piece_second,
+    piece_plane,
 ):
     z, core, y, x, nz, side = place(ndp, nf)
     dp, fs = z * 2 + core, y * side + x
@@ -1134,7 +1189,7 @@
     width_attn = held_attn.shape[-1]
     width = ffn_weight.shape[-1]
     per = width_ffn // width
-    greet(line_partners(ndp, nf))
+    greet(all_partners(ndp, nf))
 
     def place_of(turn):
         step = nf - 1 - turn
@@ -1292,6 +1347,33 @@
             def _(which=which):
                 keep(parts[:, which])
                 give(parts[:, 1 - which])
+
+    def piece_copy(matrix, half):
+        return remote(
+            ffn_low.at[matrix, half],
+            ffn_whole.at[fs, dp],
+            piece_send.at[2 * matrix + half],
+            piece_recv.at[dp],
+            (2 + 2 * matrix + half, fs),
+        )
+
+    def piece_local(matrix, half):
+        return pltpu.make_async_copy(ffn_low.at[matrix, half], ffn_whole.at[fs, dp], piece_own)
+
+    def start_pieces(matrix):
+        for half in range(2):
+            @pl.when(dp != 2 + 2 * matrix + half)
+            def _(half=half):
+                piece_copy(matrix, half).start()
+
+            @pl.when(dp == 2 + 2 * matrix + half)
+            def _(half=half):
+                piece_local(matrix, half).start(priority=1)
+
+    crossing = Crossing(
+        ndp, nf, ffn_whole, piece_own, piece_recv, piece_first, piece_second, piece_plane, ffn_low.at[0, 0]
+    )
+    runs_ffn = jnp.logical_and(dp >= 2, dp < 6)
 
     def ffn_loads(slot, turn, part):
         block = place_of(turn)
@@ -1519,16 +1601,36 @@
         pair_take(step)
     sends_at(total_steps, (total_steps,))
 
+    take_first(2, range(1, side))
+    take_z(0)
+    start_pieces(0)
+    take_z(1)
+    start_pieces(1)
     vec_take(0)
-    take_first(2, range(1, side))
     take_first(2, (0,))
+    take_second(2)
     vec_take(1)
-    take_z(0)
-    take_second(2)
+
+    @pl.when(runs_ffn)
+    def _():
+        crossing.take()
+
     vec_take(2)
-    take_z(1)
+    take_z(2)
     vec_take(3)
-    take_z(2)
+
+    @pl.when(runs_ffn)
+    def _():
+        crossing.pass_on()
+        crossing.near()
+        crossing.far()
+        crossing.finish()
+
+    for matrix in range(2):
+        for half in range(2):
+            @pl.when(dp != 2 + 2 * matrix + half)
+            def _(matrix=matrix, half=half):
+                piece_copy(matrix, half).wait_send()
 
     for chunk in range(chunks):
 
@@ -1547,7 +1649,7 @@
 
 
 def backward_kernel_entry(ndp, nf, *refs):
-    at = 18 + 7 + 12 + 2 + 2
+    at = 18 + 8 + 12 + 2 + 2
     backward_kernel(ndp, nf, *refs[:at], refs[at : at + 2], *refs[at + 2 :])
 
 
@@ -1577,6 +1679,7 @@
             jax.ShapeDtypeStruct((16, D), f32),
             jax.ShapeDtypeStruct(attn_mom.shape, bf16),
             jax.ShapeDtypeStruct((2, 2, rows, width_ffn // 2), bf16),
+            jax.ShapeDtypeStruct((nf, ndp, rows, width_ffn // 2), bf16),
         ],
         in_specs=[
             anywhere,
@@ -1598,7 +1701,7 @@
             anywhere,
             anywhere,
         ],
-        out_specs=[inside] * 7,
+        out_specs=[inside] * 7 + [anywhere],
         scratch_shapes=sums
         + [
             pltpu.VMEM((2, nz, 4, rows, width_attn), bf16),
@@ -1629,6 +1732,12 @@
             dma((3, nz - 1)),
             dma((vec_copies,)),
             dma((vec_copies,)),
+            dma,
+            dma((4,)),
+            dma((ndp,)),
+            dma((ndp, side - 1)),
+            dma((ndp, side, side - 1)),
+            dma((nf, ndp)),
         ],
         compiler_params=pltpu.CompilerParams(
             collective_id=3, has_side_effects=True, vmem_limit_bytes=63 * 1024 * 1024
@@ -1659,13 +1768,13 @@
         attn_all, up_all, down_all, blocks, active, slope, vec_full, mixture, totals, scaled, inverse, low,
         layer_out, d_second, tail_sums,
     ) = forward(ndp, nf, tokens, segments, cotangent, attn_w, ffn_w, vectors)
-    input_grad, up_grad, down_grad, attn_grad, vec_sum, attn_piece, ffn_piece = backward(
+    input_grad, up_grad, down_grad, attn_grad, vec_sum, attn_piece, _, ffn_whole = backward(
         ndp, nf, d_second, low, scaled, inverse, vec_full, active, slope, up_all, down_all,
         tokens, segments, blocks, mixture, totals, attn_all, tail_sums, attn_mom, ffn_mom,
     )
     mine = (lax.axis_index("dp") * nf + lax.axis_index("fsdp")) * share
     vec_grad = lax.dynamic_slice(vec_sum, (0, mine), (12, share))
-    attn_ortho, ffn_ortho = orthogonalize(ndp, nf, attn_piece, ffn_piece)
+    attn_ortho, ffn_ortho = orthogonalize(ndp, nf, attn_piece, ffn_whole)
     total_tokens = tokens.shape[0] * ndp * nf
     updated = update_all(
         vector_step / math.sqrt(total_tokens),

time: 434 us -> 425 us (0.979)
  Pallas kernels: 422 us -> 413 us
    pallas_call x1, Pallas kernels: 127 us -> 105 us  [orthogonalize(): pl.pallas_call(functools.partial(ortho_kernel, ndp, nf), name='newton_sch...]
    pallas_call x1, Pallas kernels: 150 us -> 164 us  [backward(): pl.pallas_call(functools.partial(backward_kernel_entry, ndp, nf), name='b...]
where the time goes in v2:
time: 425 us; the launch traced here: 418 us
  Pallas kernels  413 us (97%)
  local copies, waits for them, and re-layouts  4.93 us (1%)
    pallas_call x1, Pallas kernels, backward(): pl.pallas_call(functools.partial(backward_kernel_entry, ndp, nf), name='b...  164 us
    pallas_call x1, Pallas kernels, forward(): pl.pallas_call(functools.partial(forward_kernel, ndp, nf), name='forward'...  139 us
    pallas_call x1, Pallas kernels, orthogonalize(): pl.pallas_call(functools.partial(ortho_kernel, ndp, nf), name='newton_sch...  105 us

profile of v2, /device:TPU:25, one launch (start us, length us, event | category | flops | bytes accessed | tf_op | source)
XLA Modules:
  0.0 418.4 jit_solution(13505107916130379782)
XLA Ops:
  0.6 138.7 %forward.1 = (bf16[4,8,528,256]{3,2,1,0:T(8,128)(2,1)}, bf16[4,8,128,1024]{3,2,1,0:T(8,128)(2,1)}, bf16[4,8,128,1024]{3,2,1,0:T(8,128)(2,1)}, bf16[4,3,512,256]{...) custom-call(bf16[512,1024]{1,0:T(8,128)(2,1)} %refs_9_.1, ...), custom_call_target="tpu_custom_call" | custom-call | tf_op jit(solution)/shard_map/forward/pallas_call | solution.py:1053
  139.3 163.7 %backward.1 = (f32[512,1024]{1,0:T(8,128)}, f32[128,1024]{1,0:T(8,128)}, f32[128,1024]{1,0:T(8,128)}, f32[4,128,256]{2,1,0:T(8,128)}, f32[16,1024]{1,0:T(8,128)}...) custom-call(f32[512,1024]{1,0:T(8,128)} %get-tuple-element.46.refs_0_, ...), custom_call_target="tpu_custom_call" | custom-call | tf_op jit(solution)/shard_map/backward/pallas_call | solution.py:1673
  303.0 1.4 constant_dynamic-slice_fusion.vec_grad
  304.4 104.5 %newton_schulz.1 = (bf16[4,128,256]{2,1,0:T(8,128)(2,1)}, bf16[2,2,128,512]{3,2,1,0:T(8,128)(2,1)}) custom-call(bf16[4,128,256]{2,1,0:T(8,128)(2,1)} %get-tuple-element.65.attn_ref, bf16[4,8,128,512]{3,2,1,0:T(8,128)(2,1)} %get-tuple-element.66.ffn_whole), custom_call_target="tpu_custom_call" | custom-call | tf_op jit(solution)/shard_map/newton_schulz/pallas_call | solution.py:505
  408.9 0.0 copy-start.1
  408.9 0.0 copy-start
  408.9 5.7 %update.1 = (f32[4,128,256]{2,1,0:T(8,128)}, f32[2,128,1024]{2,1,0:T(8,128)}, f32[12,32]{1,0:T(8,128)}, f32[4,128,256]{2,1,0:T(8,128)}, f32[2,128,1024]{2,1,0:T(...) custom-call(f32[4,128,256]{2,1,0:T(8,128)} %attn_w.3, ...), custom_call_target="tpu_custom_call" | custom-call | tf_op jit(solution)/shard_map/update/pallas_call | solution.py:602
  414.6 1.3 dynamic-slice_bitcast_fusion
  415.8 0.0 copy-done.1
  415.8 1.0 copy.26
  416.8 0.0 copy-done
  416.8 1.3 copy.27
Async XLA Ops:
  408.9 6.9 %copy-start.1 = (bf16[512,1024]{1,0:T(8,128)(2,1)S(1)}, bf16[512,1024]{1,0:T(8,128)(2,1)}, u32[]{:S(2)}) copy-start(bf16[512,1024]{1,0:T(8,128)(2,1)} %get-tuple-element.90) | copy-start | bytes 3145732
  408.9 7.9 %copy-start = (f32[512,1024]{1,0:T(8,128)S(1)}, f32[512,1024]{1,0:T(8,128)}, u32[]{:S(2)}) copy-start(f32[512,1024]{1,0:T(8,128)} %get-tuple-element.91) | copy-start | bytes 6291460

commit v3 on v2

--- a/solution.py
+++ b/solution.py
@@ -691,8 +691,8 @@
     load_sem,
     store_sem,
 ):
-    chunks = 3
-    shards, wholes = (attn_shard, up_shard, down_shard), (attn_out, up_out, down_out)
+    chunks, turned = 4, 3
+    wholes = (attn_out, up_out, down_out)
     z, core, y, x, nz, side = place(ndp, nf)
     dp, fs = z * 2 + core, y * side + x
     rows, width_attn = attn_w.shape[1:]
@@ -709,8 +709,16 @@
     down_shard[...] = ffn_w[1].astype(jnp.bfloat16)
     greet(line_partners(ndp, nf))
 
+    halves = slice(0, width_ffn // 2), slice(width_ffn // 2, width_ffn)
+    shards = (attn_shard, up_shard, down_shard.at[:, halves[0]], down_shard.at[:, halves[1]])
+
+    def row_slot(chunk, plane_at, row):
+        if chunk < 2:
+            return wholes[chunk].at[plane_at, row]
+        return down_out.at[plane_at, row, :, halves[chunk - 2]]
+
     def slot(chunk, plane_at, z_at):
-        return wholes[chunk].at[plane_at, z_at * 2 + core]
+        return row_slot(chunk, plane_at, z_at * 2 + core)
 
     def source(chunk, plane_at, z_at, own):
         return shards[chunk] if own else slot(chunk, plane_at, z_at)
@@ -749,23 +757,26 @@
             (z * 2 + 1 - core, fs),
         )
 
-    def z_copy(chunk, z_at, up, own):
+    def z_copy(chunk, plane_at, z_at, up, own):
         return remote(
-            source(chunk, fs, z_at, own),
-            slot(chunk, fs, z_at),
-            z_send.at[chunk, z_at, up],
-            own_recv.at[chunk, fs, z_at],
+            source(chunk, plane_at, z_at, own),
+            slot(chunk, plane_at, z_at),
+            z_send.at[chunk, plane_at, z_at, up],
+            own_recv.at[chunk, plane_at, z_at],
             ((z + (1 if up else -1)) * 2 + core, fs),
         )
 
-    def along_z(chunk, z_at, own, act):
+    def along_z(chunk, plane_at, z_at, own, act):
         @pl.when(jnp.logical_and(z_at <= z, z < nz - 1))
         def _():
-            act(z_copy(chunk, z_at, 1, own))
+            act(z_copy(chunk, plane_at, z_at, 1, own))
 
         @pl.when(jnp.logical_and(z_at >= z, z > 0))
         def _():
-            act(z_copy(chunk, z_at, 0, own))
+            act(z_copy(chunk, plane_at, z_at, 0, own))
+
+    def begin(copy):
+        copy.start()
 
     def arrived(chunk, plane_at, z_at):
         here = slot(chunk, plane_at, z_at)
@@ -794,7 +805,7 @@
     def from_z(chunk):
         def each(z_at):
             arrived(chunk, fs, z_at)
-            along_z(chunk, z_at, False, lambda copy: copy.start())
+            along_z(chunk, fs, z_at, False, begin)
             pass_on(chunk, z_at, False)
 
         near_first(each)
@@ -828,27 +839,56 @@
         each(z)
         near_first(each)
 
+    def turned_first():
+        for line in range(1, side):
+            plane_at = along(lax.rem(z, 2) == 0, line)
+            arrived(turned, plane_at, z)
+            for step in range(1, side):
+                second_copy(turned, plane_at, z, step, False, line).start()
+            along_z(turned, plane_at, z, False, begin)
+            pair_copy(turned, plane_at, z, False).start()
+
+    def turned_second():
+        for plane_at in last_places(z):
+            arrived(turned, plane_at, z)
+            along_z(turned, plane_at, z, False, begin)
+            pair_copy(turned, plane_at, z, False).start()
+
+    def turned_z(far):
+        for z_at in (z - far, z + far):
+            @pl.when(jnp.logical_and(z_at >= 0, z_at < nz))
+            def _(z_at=z_at):
+                def each(step):
+                    plane_at = lax.rem(fs + step, nf)
+                    arrived(turned, plane_at, z_at)
+                    along_z(turned, plane_at, z_at, False, begin)
+                    pair_copy(turned, plane_at, z_at, False).start()
+
+                loop(nf, each)
+
     def from_pair(chunk):
         own_copy(chunk).wait()
 
         def each(index):
             plane_at, z_at = lax.rem(index, nf), lax.div(index, nf)
-            there = wholes[chunk].at[plane_at, z_at * 2 + 1 - core]
+            there = row_slot(chunk, plane_at, z_at * 2 + 1 - core)
             remote(
                 there, there, own_sem.at[chunk], pair_recv.at[chunk, plane_at, z_at], (dp, fs)
             ).wait_recv()
 
         loop(nf * nz, each)
 
-    for chunk in range(chunks):
+    for chunk in (0, turned, 1, 2):
         own_copy(chunk).start(priority=1)
-        along_z(chunk, z, True, lambda copy: copy.start())
+        along_z(chunk, fs, z, True, begin)
         pass_on(chunk, z, True)
 
     from_z(0)
     from_first(0)
+    turned_first()
     from_z(1)
     from_second(0)
+    turned_second()
     from_pair(0)
 
     def load(index, source, target):
@@ -925,10 +965,12 @@
         @pl.when(block == 0)
         def _():
             from_z(2)
+            turned_z(1)
 
         @pl.when(block == nf - 2)
         def _():
             from_first(1)
+            turned_z(2)
 
     loop(nf, attn_turn)
 
@@ -993,6 +1035,11 @@
         total[...] += contract_cols(active[step], flat(ffn_weight[at]))
 
     def between_up(step):
+        @pl.when(step == 0)
+        def _():
+            for far in range(3, nz):
+                turned_z(far)
+
         @pl.when(step == FF // width // 2)
         def _():
             from_first(2)
@@ -1004,6 +1051,7 @@
         copy.wait()
     from_second(2)
     from_pair(2)
+    from_pair(turned)
     ffn_steps(2, down_step, lambda step: None)
     sums_out[...] = jnp.zeros((8, D), jnp.float32)
 
@@ -1026,14 +1074,22 @@
     loop(nf, stored)
     for chunk in range(chunks):
         def finish(z_at):
-            along_z(chunk, z_at, False, lambda copy: copy.wait_send())
-            for step in range(1, side):
-                first_copy(chunk, z_at, step, False).wait_send()
-                for line in range(side):
-                    second_copy(chunk, fs, z_at, step, False, line).wait_send()
+            def sent():
+                for step in range(1, side):
+                    first_copy(chunk, z_at, step, False).wait_send()
+                    for line in range(side):
+                        second_copy(chunk, fs, z_at, step, False, line).wait_send()
+
+            if chunk == turned:
+                pl.when(z_at == z)(sent)
+            else:
+                sent()
+                along_z(chunk, fs, z_at, False, lambda copy: copy.wait_send())
 
             def each(plane_at):
                 pair_copy(chunk, plane_at, z_at, False).wait_send()
+                if chunk == turned:
+                    along_z(chunk, plane_at, z_at, False, lambda copy: copy.wait_send())
 
             loop(nf, each)
 
@@ -1041,7 +1097,7 @@
 
 
 def forward(ndp, nf, tokens, segments, cotangent, attn_w, ffn_w, vectors):
-    nz, side, chunks = ndp // 2, math.isqrt(nf), 3
+    nz, side, chunks = ndp // 2, math.isqrt(nf), 4
     count = tokens.shape[0]
     rows, width_attn = attn_w.shape[1:]
     width_ffn = ffn_w.shape[2]
@@ -1090,7 +1146,7 @@
             dma((chunks,)),
             dma((chunks, nf, nz)),
             dma((chunks, nf, nz)),
-            dma((chunks, nz, 2)),
+            dma((chunks, nf, nz, 2)),
             dma((chunks, nz, side - 1)),
             dma((chunks, nz, side, side - 1)),
             dma((chunks, nf, nz)),

time: 425 us -> 416 us (0.979)
  Pallas kernels: 413 us -> 403 us
    pallas_call x1, Pallas kernels: 139 us -> 128 us  [forward(): pl.pallas_call(functools.partial(forward_kernel, ndp, nf), name='forward'...]
where the time goes in v3:
time: 416 us; the launch traced here: 409 us
  Pallas kernels  403 us (97%)
  local copies, waits for them, and re-layouts  4.93 us (1%)
    pallas_call x1, Pallas kernels, backward(): pl.pallas_call(functools.partial(backward_kernel_entry, ndp, nf), name='b...  165 us
    pallas_call x1, Pallas kernels, forward(): pl.pallas_call(functools.partial(forward_kernel, ndp, nf), name='forward'...  128 us
    pallas_call x1, Pallas kernels, orthogonalize(): pl.pallas_call(functools.partial(ortho_kernel, ndp, nf), name='newton_sch...  104 us

profile of v3, /device:TPU:25, one launch (start us, length us, event | category | flops | bytes accessed | tf_op | source)
XLA Modules:
  0.0 409.2 jit_solution(2141171086804898384)
XLA Ops:
  0.6 127.9 %forward.1 = (bf16[4,8,528,256]{3,2,1,0:T(8,128)(2,1)}, bf16[4,8,128,1024]{3,2,1,0:T(8,128)(2,1)}, bf16[4,8,128,1024]{3,2,1,0:T(8,128)(2,1)}, bf16[4,3,512,256]{...) custom-call(bf16[512,1024]{1,0:T(8,128)(2,1)} %refs_9_.1, ...), custom_call_target="tpu_custom_call" | custom-call | tf_op jit(solution)/shard_map/forward/pallas_call | solution.py:1109
  128.5 165.3 %backward.1 = (f32[512,1024]{1,0:T(8,128)}, f32[128,1024]{1,0:T(8,128)}, f32[128,1024]{1,0:T(8,128)}, f32[4,128,256]{2,1,0:T(8,128)}, f32[16,1024]{1,0:T(8,128)}...) custom-call(f32[512,1024]{1,0:T(8,128)} %get-tuple-element.46.refs_0_, ...), custom_call_target="tpu_custom_call" | custom-call | tf_op jit(solution)/shard_map/backward/pallas_call | solution.py:1729
  293.9 1.4 constant_dynamic-slice_fusion.vec_grad
  295.2 104.5 %newton_schulz.1 = (bf16[4,128,256]{2,1,0:T(8,128)(2,1)}, bf16[2,2,128,512]{3,2,1,0:T(8,128)(2,1)}) custom-call(bf16[4,128,256]{2,1,0:T(8,128)(2,1)} %get-tuple-element.65.attn_ref, bf16[4,8,128,512]{3,2,1,0:T(8,128)(2,1)} %get-tuple-element.66.ffn_whole), custom_call_target="tpu_custom_call" | custom-call | tf_op jit(solution)/shard_map/newton_schulz/pallas_call | solution.py:505
  399.7 0.0 copy-start.1
  399.7 0.0 copy-start
  399.7 5.7 %update.1 = (f32[4,128,256]{2,1,0:T(8,128)}, f32[2,128,1024]{2,1,0:T(8,128)}, f32[12,32]{1,0:T(8,128)}, f32[4,128,256]{2,1,0:T(8,128)}, f32[2,128,1024]{2,1,0:T(...) custom-call(f32[4,128,256]{2,1,0:T(8,128)} %attn_w.3, ...), custom_call_target="tpu_custom_call" | custom-call | tf_op jit(solution)/shard_map/update/pallas_call | solution.py:602
  405.4 1.3 dynamic-slice_bitcast_fusion
  406.6 0.0 copy-done.1
  406.7 1.0 copy.26
  407.6 0.0 copy-done
  407.6 1.3 copy.27
Async XLA Ops:
  399.7 6.9 %copy-start.1 = (bf16[512,1024]{1,0:T(8,128)(2,1)S(1)}, bf16[512,1024]{1,0:T(8,128)(2,1)}, u32[]{:S(2)}) copy-start(bf16[512,1024]{1,0:T(8,128)(2,1)} %get-tuple-element.90) | copy-start | bytes 3145732
  399.7 7.9 %copy-start = (f32[512,1024]{1,0:T(8,128)S(1)}, f32[512,1024]{1,0:T(8,128)}, u32[]{:S(2)}) copy-start(f32[512,1024]{1,0:T(8,128)} %get-tuple-element.91) | copy-start | bytes 6291460

commit v4 on v3

--- a/solution.py
+++ b/solution.py
@@ -1200,6 +1200,9 @@
     z_up,
     z_down,
     z_attn,
+    first_turned,
+    second_turned,
+    z_turned,
     stages_out,
     land,
     ffn_weight,
@@ -1233,15 +1236,19 @@
     piece_first,
     piece_second,
     piece_plane,
+    turned_send,
+    turned_recv,
 ):
     z, core, y, x, nz, side = place(ndp, nf)
     dp, fs = z * 2 + core, y * side + x
     other = (z * 2 + 1 - core, fs)
+    chunks, turned = 3, 3
+    rows, width_ffn = held_up.shape[2:]
+    half_width = width_ffn // 2
     held, outs = (held_up, held_down, held_attn), (up_out, down_out, attn_out)
-    from_first, from_second = (first_up, first_down, first_attn), (second_up, second_down, second_attn)
+    from_first = (first_up, first_down, first_attn, first_turned)
+    from_second = (second_up, second_down, second_attn, second_turned)
     from_z = (z_up, z_down, z_attn)
-    chunks = 3
-    rows, width_ffn = held_up.shape[2:]
     width_attn = held_attn.shape[-1]
     width = ffn_weight.shape[-1]
     per = width_ffn // width
@@ -1250,6 +1257,22 @@
     def place_of(turn):
         step = nf - 1 - turn
         return lax.rem(y + lax.div(step, side), side) * side + lax.rem(x + lax.rem(step, side), side)
+
+    def sums(chunk, z_at, plane_at):
+        if chunk == 1:
+            return held_down.at[z_at, plane_at, :, pl.ds(0, half_width)]
+        if chunk == turned:
+            return held_down.at[z_at, plane_at, :, pl.ds(half_width, half_width)]
+        return held[chunk].at[z_at, plane_at]
+
+    def add(target, source):
+        target[...] = target[...] + source[...]
+
+    def first_land(chunk, z_at, step, line):
+        return from_first[chunk].at[0 if chunk == turned else z_at, step - 1, line]
+
+    def second_land(chunk, z_at, step):
+        return from_second[chunk].at[0 if chunk == turned else z_at, step - 1]
 
     def first_copy(chunk, z_at, line, step):
         x_first = lax.rem(z_at, 2) == 0
@@ -1261,8 +1284,8 @@
             far * side + lax.rem(x + line, side),
         )
         return remote(
-            held[chunk].at[z_at, at],
-            from_first[chunk].at[z_at, step - 1, line],
+            sums(chunk, z_at, at),
+            first_land(chunk, z_at, step, line),
             first_send.at[chunk, z_at, step - 1, line],
             first_recv.at[chunk, z_at, step - 1, line],
             (dp, to),
@@ -1277,7 +1300,7 @@
             for z_at in range(0, nz, 2):
                 schedule.setdefault(ready, []).extend((chunk, turns, z_at) for chunk in sent)
 
-    def send_first(chunk, turns, z_from):
+    def send_first(chunk, turns, z_from, z_count=2):
         def each(z_at):
             x_first = lax.rem(z_at, 2) == 0
             for turn in turns:
@@ -1289,7 +1312,7 @@
                 def _(line=line, step=step):
                     first_copy(chunk, z_at, line, step).start()
 
-        loop(z_from + 2, each, z_from)
+        loop(z_from + z_count, each, z_from)
 
     def sends_at(step, steps):
         for when in steps:
@@ -1307,8 +1330,8 @@
     def second_copy(chunk, z_at, step):
         to = line_place(z_at, step)
         return remote(
-            held[chunk].at[z_at, to],
-            from_second[chunk].at[z_at, step - 1],
+            sums(chunk, z_at, to),
+            second_land(chunk, z_at, step),
             second_send.at[chunk, z_at, step - 1],
             second_recv.at[chunk, z_at, step - 1],
             (dp, to),
@@ -1317,7 +1340,7 @@
     def z_copy(chunk, step):
         z_at = lax.rem(z + step, nz)
         return remote(
-            held[chunk].at[z_at, fs],
+            sums(chunk, z_at, fs),
             from_z[chunk].at[step - 1],
             z_send.at[chunk, step - 1],
             z_recv.at[chunk, step - 1],
@@ -1331,18 +1354,44 @@
                 at = line_place(z_at, line)
                 for step in range(1, side):
                     first_copy(chunk, z_at, line, step).wait_recv()
-                    held[chunk][z_at, at] += from_first[chunk][z_at, step - 1, line]
+                    add(sums(chunk, z_at, at), first_land(chunk, z_at, step, line))
                 if line:
                     second_copy(chunk, z_at, line).start()
 
-        loop(nz, each)
+        if chunk == turned:
+            each(nz - 1)
+        else:
+            loop(nz, each)
+
+    def turned_copy(plane_at, step):
+        z_at = lax.rem(z + step, nz)
+        return remote(
+            sums(turned, z_at, plane_at),
+            z_turned.at[step - 1, plane_at],
+            turned_send.at[step - 1, plane_at],
+            turned_recv.at[step - 1, plane_at],
+            (z_at * 2 + core, fs),
+        )
+
+    def turned_start(turns):
+        for turn in turns:
+            for step in range(1, nz):
+                turned_copy(place_of(turn), step).start()
+
+    def turned_take(turns):
+        for turn in turns:
+            plane_at = place_of(turn)
+            for step in range(1, nz):
+                turned_copy(plane_at, step).wait_recv()
+                add(sums(turned, z, plane_at), z_turned.at[step - 1, plane_at])
+        send_first(turned, turns, z, 1)
 
     def take_second(chunk):
         def each(hop):
             z_at = lax.rem(z + 1 + hop, nz)
             for step in range(1, side):
                 second_copy(chunk, z_at, step).wait_recv()
-                held[chunk][z_at, fs] += from_second[chunk][z_at, step - 1]
+                add(sums(chunk, z_at, fs), second_land(chunk, z_at, step))
 
             @pl.when(hop < nz - 1)
             def _():
@@ -1355,19 +1404,27 @@
         return pltpu.make_async_copy(source, outs[chunk], load_sem.at[3 + chunk])
 
     def take_z(chunk):
-        total = held[chunk][z, fs].astype(jnp.float32)
+        moments(chunk).wait()
+        total = sums(chunk, z, fs)[...].astype(jnp.float32)
         for step in range(1, nz):
             z_copy(chunk, step).wait_recv()
             total += from_z[chunk][step - 1].astype(jnp.float32)
-        moments(chunk).wait()
-        low = (matrix_decay * outs[chunk][...] + total).astype(jnp.bfloat16)
-        outs[chunk][...] = total
-        if chunk < 2:
-            half = low.shape[1] // 2
-            ffn_low[chunk, 0] = low[:, :half]
-            ffn_low[chunk, 1] = low[:, half:]
+        if chunk == 0:
+            low = (matrix_decay * up_out[...] + total).astype(jnp.bfloat16)
+            up_out[...] = total
+            ffn_low[0, 0] = low[:, :half_width]
+            ffn_low[0, 1] = low[:, half_width:]
+        elif chunk == 1:
+            for step in range(1, side):
+                second_copy(turned, z, step).wait_recv()
+                add(sums(turned, z, fs), second_land(turned, z, step))
+            for index, value in enumerate((total, sums(turned, z, fs)[...].astype(jnp.float32))):
+                at = slice(index * half_width, (index + 1) * half_width)
+                ffn_low[1, index] = (matrix_decay * down_out[:, at] + value).astype(jnp.bfloat16)
+                down_out[:, at] = value
         else:
-            attn_low[...] = low
+            attn_low[...] = (matrix_decay * attn_out[...] + total).astype(jnp.bfloat16)
+            attn_out[...] = total
 
     vec_rounds = [[other]]
     vec_rounds.append([(dp, y * side + lax.rem(x + step, side)) for step in range(1, side)])
@@ -1512,6 +1569,14 @@
                 pair_take(now - lag)
 
             sends_at(now, range(nf * per))
+
+            @pl.when(now == per - 1 + lag)
+            def _():
+                turned_start((0,))
+
+            @pl.when(now == (nf - 1) * per - 1 + lag)
+            def _():
+                turned_start(range(1, nf - 1))
             at = slice(part * width, (part + 1) * width)
             for index in range(2):
 
@@ -1617,7 +1682,7 @@
 
         pair_take(now - lag)
         for index in range(4):
-            turned, grad = (turned_one, grads[index]) if index < 3 else (turned_two, branch[block])
+            flipped, grad = (turned_one, grads[index]) if index < 3 else (turned_two, branch[block])
 
             def keep(values, index=index):
                 held_attn[:, block, index] = values
@@ -1625,19 +1690,34 @@
             def give(values, index=index):
                 stages_out[lax.rem(now, lag), :, index] = values
 
-            split(product(turned[...], grad), keep, give)
+            split(product(flipped[...], grad), keep, give)
         pair_copy(now).start()
         sends_at(now, range(nf * per, total_steps))
 
         @pl.when(turn == nf - 4)
         def _():
+            turned_take((0,))
             take_first(0, range(1, side))
             take_first(1, range(1, side))
 
+        @pl.when(turn == lag - 1)
+        def _():
+            turned_start((nf - 1,))
+
         @pl.when(turn == nf - 3)
         def _():
+            turned_take(range(1, nf - 1))
             take_first(0, (0,))
             take_first(1, (0,))
+
+        @pl.when(turn == nf - 2)
+        def _():
+            take_first(turned, range(1, side))
+
+        @pl.when(turn == nf - 1)
+        def _():
+            turned_take((nf - 1,))
+            take_first(turned, (0,))
 
         @pl.when(turn == nf - 2)
         def _():
@@ -1688,6 +1768,15 @@
             def _(matrix=matrix, half=half):
                 piece_copy(matrix, half).wait_send()
 
+    def turned_sent(plane_at):
+        for step in range(1, nz):
+            turned_copy(plane_at, step).wait_send()
+
+    loop(nf, turned_sent)
+    for step in range(1, side):
+        second_copy(turned, z, step).wait_send()
+        for line in range(side):
+            first_copy(turned, z, line, step).wait_send()
     for chunk in range(chunks):
 
         def finish(z_at):
@@ -1705,7 +1794,7 @@
 
 
 def backward_kernel_entry(ndp, nf, *refs):
-    at = 18 + 8 + 12 + 2 + 2
+    at = 18 + 8 + 15 + 2 + 2
     backward_kernel(ndp, nf, *refs[:at], refs[at : at + 2], *refs[at + 2 :])
 
 
@@ -1723,9 +1812,11 @@
     anywhere, inside = pl.BlockSpec(memory_space=pl.ANY), pl.BlockSpec(memory_space=pltpu.VMEM)
     shapes = [(rows, width_ffn), (rows, width_ffn), (4, rows, width_attn)]
     vec_copies = 1 + 2 * (side - 1) + nz - 1
-    sums = []
-    for lead in ((nz, nf), (nz, side - 1, side), (nz, side - 1), (nz - 1,)):
-        sums += [pltpu.VMEM(lead + shape, bf16) for shape in shapes]
+    half = (rows, width_ffn // 2)
+    sums = [pltpu.VMEM((nz, nf) + shape, bf16) for shape in shapes]
+    for lead in ((nz, side - 1, side), (nz, side - 1), (nz - 1,)):
+        sums += [pltpu.VMEM(lead + shape, bf16) for shape in (shapes[0], half, shapes[2])]
+    sums += [pltpu.VMEM(lead + half, bf16) for lead in ((1, side - 1, side), (1, side - 1), (nz - 1, nf))]
     return pl.pallas_call(
         functools.partial(backward_kernel_entry, ndp, nf),
         name="backward",
@@ -1780,10 +1871,10 @@
             dma((2, 4)),
             dma((2,)),
             dma((4,)),
-            dma((3, nz, side - 1, side)),
-            dma((3, nz, side - 1, side)),
-            dma((3, nz, side - 1)),
-            dma((3, nz, side - 1)),
+            dma((4, nz, side - 1, side)),
+            dma((4, nz, side - 1, side)),
+            dma((4, nz, side - 1)),
+            dma((4, nz, side - 1)),
             dma((3, nz - 1)),
             dma((3, nz - 1)),
             dma((vec_copies,)),
@@ -1794,6 +1885,8 @@
             dma((ndp, side - 1)),
             dma((ndp, side, side - 1)),
             dma((nf, ndp)),
+            dma((nz - 1, nf)),
+            dma((nz - 1, nf)),
         ],
         compiler_params=pltpu.CompilerParams(
             collective_id=3, has_side_effects=True, vmem_limit_bytes=63 * 1024 * 1024

time: 416 us -> 399 us (0.959)
  Pallas kernels: 403 us -> 387 us
    pallas_call x1, Pallas kernels: 165 us -> 147 us  [backward(): pl.pallas_call(functools.partial(backward_kernel_entry, ndp, nf), name='b...]
where the time goes in v4:
time: 399 us; the launch traced here: 392 us
  Pallas kernels  387 us (97%)
  local copies, waits for them, and re-layouts  4.93 us (1%)
    pallas_call x1, Pallas kernels, backward(): pl.pallas_call(functools.partial(backward_kernel_entry, ndp, nf), name='b...  147 us
    pallas_call x1, Pallas kernels, forward(): pl.pallas_call(functools.partial(forward_kernel, ndp, nf), name='forward'...  128 us
    pallas_call x1, Pallas kernels, orthogonalize(): pl.pallas_call(functools.partial(ortho_kernel, ndp, nf), name='newton_sch...  106 us

profile of v4, /device:TPU:25, one launch (start us, length us, event | category | flops | bytes accessed | tf_op | source)
XLA Modules:
  0.0 392.4 jit_solution(7363978257631700015)
XLA Ops:
  0.6 127.9 %forward.1 = (bf16[4,8,528,256]{3,2,1,0:T(8,128)(2,1)}, bf16[4,8,128,1024]{3,2,1,0:T(8,128)(2,1)}, bf16[4,8,128,1024]{3,2,1,0:T(8,128)(2,1)}, bf16[4,3,512,256]{...) custom-call(bf16[512,1024]{1,0:T(8,128)(2,1)} %refs_9_.1, ...), custom_call_target="tpu_custom_call" | custom-call | tf_op jit(solution)/shard_map/forward/pallas_call | solution.py:1109
  128.5 147.4 %backward.1 = (f32[512,1024]{1,0:T(8,128)}, f32[128,1024]{1,0:T(8,128)}, f32[128,1024]{1,0:T(8,128)}, f32[4,128,256]{2,1,0:T(8,128)}, f32[16,1024]{1,0:T(8,128)}...) custom-call(f32[512,1024]{1,0:T(8,128)} %get-tuple-element.46.refs_0_, ...), custom_call_target="tpu_custom_call" | custom-call | tf_op jit(solution)/shard_map/backward/pallas_call | solution.py:1820
  275.9 1.4 constant_dynamic-slice_fusion.vec_grad
  277.3 105.6 %newton_schulz.1 = (bf16[4,128,256]{2,1,0:T(8,128)(2,1)}, bf16[2,2,128,512]{3,2,1,0:T(8,128)(2,1)}) custom-call(bf16[4,128,256]{2,1,0:T(8,128)(2,1)} %get-tuple-element.65.attn_ref, bf16[4,8,128,512]{3,2,1,0:T(8,128)(2,1)} %get-tuple-element.66.ffn_whole), custom_call_target="tpu_custom_call" | custom-call | tf_op jit(solution)/shard_map/newton_schulz/pallas_call | solution.py:505
  382.9 0.0 copy-start.1
  382.9 0.0 copy-start
  382.9 5.7 %update.1 = (f32[4,128,256]{2,1,0:T(8,128)}, f32[2,128,1024]{2,1,0:T(8,128)}, f32[12,32]{1,0:T(8,128)}, f32[4,128,256]{2,1,0:T(8,128)}, f32[2,128,1024]{2,1,0:T(...) custom-call(f32[4,128,256]{2,1,0:T(8,128)} %attn_w.3, ...), custom_call_target="tpu_custom_call" | custom-call | tf_op jit(solution)/shard_map/update/pallas_call | solution.py:602
  388.6 1.3 dynamic-slice_bitcast_fusion
  389.8 0.0 copy-done.1
  389.9 1.0 copy.26
  390.8 0.0 copy-done
  390.8 1.3 copy.27
Async XLA Ops:
  382.9 6.9 %copy-start.1 = (bf16[512,1024]{1,0:T(8,128)(2,1)S(1)}, bf16[512,1024]{1,0:T(8,128)(2,1)}, u32[]{:S(2)}) copy-start(bf16[512,1024]{1,0:T(8,128)(2,1)} %get-tuple-element.90) | copy-start | bytes 3145732
  382.9 7.9 %copy-start = (f32[512,1024]{1,0:T(8,128)S(1)}, f32[512,1024]{1,0:T(8,128)}, u32[]{:S(2)}) copy-start(f32[512,1024]{1,0:T(8,128)} %get-tuple-element.91) | copy-start | bytes 6291460

commit v5 on v4

--- a/solution.py
+++ b/solution.py
@@ -992,21 +992,22 @@
         left = pl.multiple_of(part * width, width)
         return load(5 + at, wholes[chunk].at[block, :, :, pl.ds(left, width)], ffn_weight.at[at])
 
-    def ffn_steps(chunk, body, between):
-        ffn_load(chunk, 0, 0).start(priority=1)
-
-        def each(step):
-            at = lax.rem(step, 2)
-
-            @pl.when(step < FF // width - 1)
+    def ffn_steps(chunk, body, between, first=0, stride=1):
+        ffn_load(chunk, first, 0).start(priority=1)
+        count_steps = FF // width // stride
+
+        def each(index):
+            at, step = lax.rem(index, 2), first + index * stride
+
+            @pl.when(index < count_steps - 1)
             def _():
-                ffn_load(chunk, step + 1, 1 - at).start(priority=1)
+                ffn_load(chunk, step + stride, 1 - at).start(priority=1)
 
             ffn_load(chunk, step, at).wait()
             body(step, at)
             between(step)
 
-        loop(FF // width, each)
+        loop(count_steps, each)
 
     def keep(step):
         column = pl.ds(pl.multiple_of(step * width, width), width)
@@ -1050,9 +1051,10 @@
     for copy in keep(FF // width - 1):
         copy.wait()
     from_second(2)
+    from_pair(turned)
+    ffn_steps(2, down_step, lambda step: None, 1, 2)
     from_pair(2)
-    from_pair(turned)
-    ffn_steps(2, down_step, lambda step: None)
+    ffn_steps(2, down_step, lambda step: None, 0, 2)
     sums_out[...] = jnp.zeros((8, D), jnp.float32)
 
     def second_norm(index):
@@ -1101,7 +1103,7 @@
     count = tokens.shape[0]
     rows, width_attn = attn_w.shape[1:]
     width_ffn = ffn_w.shape[2]
-    width = min(512, width_ffn)
+    width = width_ffn // 2
     bf16, f32 = jnp.bfloat16, jnp.float32
     dma = pltpu.SemaphoreType.DMA
     anywhere, inside = pl.BlockSpec(memory_space=pl.ANY), pl.BlockSpec(memory_space=pltpu.VMEM)
@@ -1291,7 +1293,7 @@
             (dp, to),
         )
 
-    lag = 2
+    lag = 1
     total_steps = nf * per + nf
     schedule = {}
     for sent, base, stride in (((0, 1), 0, per), ((2,), nf * per, 1)):
@@ -1694,15 +1696,15 @@
         pair_copy(now).start()
         sends_at(now, range(nf * per, total_steps))
 
+        @pl.when(turn == lag - 1)
+        def _():
+            turned_start((nf - 1,))
+
         @pl.when(turn == nf - 4)
         def _():
             turned_take((0,))
             take_first(0, range(1, side))
             take_first(1, range(1, side))
-
-        @pl.when(turn == lag - 1)
-        def _():
-            turned_start((nf - 1,))
 
         @pl.when(turn == nf - 3)
         def _():
@@ -1851,8 +1853,8 @@
         out_specs=[inside] * 7 + [anywhere],
         scratch_shapes=sums
         + [
+            pltpu.VMEM((1, nz, 4, rows, width_attn), bf16),
             pltpu.VMEM((2, nz, 4, rows, width_attn), bf16),
-            pltpu.VMEM((4, nz, 4, rows, width_attn), bf16),
             pltpu.VMEM((2, 2, ndp, rows, width), bf16),
             pltpu.VMEM((2, 2, count, width), bf16),
             pltpu.VMEM((ndp, 3 * rows, width_attn), bf16),
@@ -1869,8 +1871,8 @@
             pltpu.VMEM((4 + vec_copies, 16, D), f32),
             dma((6,)),
             dma((2, 4)),
+            dma((1,)),
             dma((2,)),
-            dma((4,)),
             dma((4, nz, side - 1, side)),
             dma((4, nz, side - 1, side)),
             dma((4, nz, side - 1)),

time: 399 us -> 402 us (level)
  no operation moved by 1% of the time
where the time goes in v5:
time: 402 us; the launch traced here: 395 us
  Pallas kernels  389 us (97%)
  local copies, waits for them, and re-layouts  4.93 us (1%)
    pallas_call x1, Pallas kernels, backward(): pl.pallas_call(functools.partial(backward_kernel_entry, ndp, nf), name='b...  150 us
    pallas_call x1, Pallas kernels, forward(): pl.pallas_call(functools.partial(forward_kernel, ndp, nf), name='forward'...  129 us
    pallas_call x1, Pallas kernels, orthogonalize(): pl.pallas_call(functools.partial(ortho_kernel, ndp, nf), name='newton_sch...  105 us

profile of v5, /device:TPU:25, one launch (start us, length us, event | category | flops | bytes accessed | tf_op | source)
XLA Modules:
  0.0 394.8 jit_solution(16305200268033465663)
XLA Ops:
  0.6 128.6 %forward.1 = (bf16[4,8,528,256]{3,2,1,0:T(8,128)(2,1)}, bf16[4,8,128,1024]{3,2,1,0:T(8,128)(2,1)}, bf16[4,8,128,1024]{3,2,1,0:T(8,128)(2,1)}, bf16[4,3,512,256]{...) custom-call(bf16[512,1024]{1,0:T(8,128)(2,1)} %refs_9_.1, ...), custom_call_target="tpu_custom_call" | custom-call | tf_op jit(solution)/shard_map/forward/pallas_call | solution.py:1111
  129.2 149.8 %backward.1 = (f32[512,1024]{1,0:T(8,128)}, f32[128,1024]{1,0:T(8,128)}, f32[128,1024]{1,0:T(8,128)}, f32[4,128,256]{2,1,0:T(8,128)}, f32[16,1024]{1,0:T(8,128)}...) custom-call(f32[512,1024]{1,0:T(8,128)} %get-tuple-element.46.refs_0_, ...), custom_call_target="tpu_custom_call" | custom-call | tf_op jit(solution)/shard_map/backward/pallas_call | solution.py:1822
  279.0 1.4 constant_dynamic-slice_fusion.vec_grad
  280.4 105.0 %newton_schulz.1 = (bf16[4,128,256]{2,1,0:T(8,128)(2,1)}, bf16[2,2,128,512]{3,2,1,0:T(8,128)(2,1)}) custom-call(bf16[4,128,256]{2,1,0:T(8,128)(2,1)} %get-tuple-element.65.attn_ref, bf16[4,8,128,512]{3,2,1,0:T(8,128)(2,1)} %get-tuple-element.66.ffn_whole), custom_call_target="tpu_custom_call" | custom-call | tf_op jit(solution)/shard_map/newton_schulz/pallas_call | solution.py:505
  385.3 0.0 copy-start.1
  385.3 0.0 copy-start
  385.4 5.7 %update.1 = (f32[4,128,256]{2,1,0:T(8,128)}, f32[2,128,1024]{2,1,0:T(8,128)}, f32[12,32]{1,0:T(8,128)}, f32[4,128,256]{2,1,0:T(8,128)}, f32[2,128,1024]{2,1,0:T(...) custom-call(f32[4,128,256]{2,1,0:T(8,128)} %attn_w.3, ...), custom_call_target="tpu_custom_call" | custom-call | tf_op jit(solution)/shard_map/update/pallas_call | solution.py:602
  391.0 1.3 dynamic-slice_bitcast_fusion
  392.3 0.0 copy-done.1
  392.3 1.0 copy.26
  393.2 0.0 copy-done
  393.2 1.3 copy.27
Async XLA Ops:
  385.3 6.9 %copy-start.1 = (bf16[512,1024]{1,0:T(8,128)(2,1)S(1)}, bf16[512,1024]{1,0:T(8,128)(2,1)}, u32[]{:S(2)}) copy-start(bf16[512,1024]{1,0:T(8,128)(2,1)} %get-tuple-element.90) | copy-start | bytes 3145732
  385.3 7.9 %copy-start = (f32[512,1024]{1,0:T(8,128)S(1)}, f32[512,1024]{1,0:T(8,128)}, u32[]{:S(2)}) copy-start(f32[512,1024]{1,0:T(8,128)} %get-tuple-element.91) | copy-start | bytes 6291460

commit v6 on v5

--- a/solution.py
+++ b/solution.py
@@ -1293,12 +1293,12 @@
             (dp, to),
         )
 
-    lag = 1
+    lag = 2
     total_steps = nf * per + nf
     schedule = {}
-    for sent, base, stride in (((0, 1), 0, per), ((2,), nf * per, 1)):
+    for sent, base, stride, late in (((0, 1), 0, per, lag), ((2,), nf * per, 1, 1)):
         for turns in ((0,), tuple(range(1, nf - 1))):
-            ready = min(base + (turns[-1] + 1) * stride - 1 + lag, total_steps)
+            ready = min(base + (turns[-1] + 1) * stride - 1 + late, total_steps)
             for z_at in range(0, nz, 2):
                 schedule.setdefault(ready, []).extend((chunk, turns, z_at) for chunk in sent)
 
@@ -1682,7 +1682,11 @@
         input_grad[...] += moved
         load_next(0)
 
-        pair_take(now - lag)
+        @pl.when(turn == 0)
+        def _():
+            pair_take(now - 2)
+
+        pair_take(now - 1)
         for index in range(4):
             flipped, grad = (turned_one, grads[index]) if index < 3 else (turned_two, branch[block])
 
@@ -1696,7 +1700,7 @@
         pair_copy(now).start()
         sends_at(now, range(nf * per, total_steps))
 
-        @pl.when(turn == lag - 1)
+        @pl.when(turn == 0)
         def _():
             turned_start((nf - 1,))
 
@@ -1735,8 +1739,7 @@
         left = index * width
         vec_land[0, 5 + left // D : 6 + left // D, left % D : left % D + width] = bias_up_sum[index]
     vec_start(0)
-    for step in range(total_steps - lag, total_steps):
-        pair_take(step)
+    pair_take(total_steps - 1)
     sends_at(total_steps, (total_steps,))
 
     take_first(2, range(1, side))
@@ -1853,8 +1856,8 @@
         out_specs=[inside] * 7 + [anywhere],
         scratch_shapes=sums
         + [
-            pltpu.VMEM((1, nz, 4, rows, width_attn), bf16),
             pltpu.VMEM((2, nz, 4, rows, width_attn), bf16),
+            pltpu.VMEM((4, nz, 4, rows, width_attn), bf16),
             pltpu.VMEM((2, 2, ndp, rows, width), bf16),
             pltpu.VMEM((2, 2, count, width), bf16),
             pltpu.VMEM((ndp, 3 * rows, width_attn), bf16),
@@ -1871,8 +1874,8 @@
             pltpu.VMEM((4 + vec_copies, 16, D), f32),
             dma((6,)),
             dma((2, 4)),
-            dma((1,)),
             dma((2,)),
+            dma((4,)),
             dma((4, nz, side - 1, side)),
             dma((4, nz, side - 1, side)),
             dma((4, nz, side - 1)),

time: 402 us -> 401 us (level)
  no operation moved by 1% of the time
where the time goes in v6:
time: 401 us; the launch traced here: 394 us
  Pallas kernels  388 us (97%)
  local copies, waits for them, and re-layouts  4.93 us (1%)
    pallas_call x1, Pallas kernels, backward(): pl.pallas_call(functools.partial(backward_kernel_entry, ndp, nf), name='b...  146 us
    pallas_call x1, Pallas kernels, forward(): pl.pallas_call(functools.partial(forward_kernel, ndp, nf), name='forward'...  129 us
    pallas_call x1, Pallas kernels, orthogonalize(): pl.pallas_call(functools.partial(ortho_kernel, ndp, nf), name='newton_sch...  108 us

profile of v6, /device:TPU:25, one launch (start us, length us, event | category | flops | bytes accessed | tf_op | source)
XLA Modules:
  0.0 393.8 jit_solution(5712687740455110912)
XLA Ops:
  0.6 128.6 %forward.1 = (bf16[4,8,528,256]{3,2,1,0:T(8,128)(2,1)}, bf16[4,8,128,1024]{3,2,1,0:T(8,128)(2,1)}, bf16[4,8,128,1024]{3,2,1,0:T(8,128)(2,1)}, bf16[4,3,512,256]{...) custom-call(bf16[512,1024]{1,0:T(8,128)(2,1)} %refs_9_.1, ...), custom_call_target="tpu_custom_call" | custom-call | tf_op jit(solution)/shard_map/forward/pallas_call | solution.py:1111
  129.2 145.8 %backward.1 = (f32[512,1024]{1,0:T(8,128)}, f32[128,1024]{1,0:T(8,128)}, f32[128,1024]{1,0:T(8,128)}, f32[4,128,256]{2,1,0:T(8,128)}, f32[16,1024]{1,0:T(8,128)}...) custom-call(f32[512,1024]{1,0:T(8,128)} %get-tuple-element.46.refs_0_, ...), custom_call_target="tpu_custom_call" | custom-call | tf_op jit(solution)/shard_map/backward/pallas_call | solution.py:1825
  275.0 1.4 constant_dynamic-slice_fusion.vec_grad
  276.4 107.8 %newton_schulz.1 = (bf16[4,128,256]{2,1,0:T(8,128)(2,1)}, bf16[2,2,128,512]{3,2,1,0:T(8,128)(2,1)}) custom-call(bf16[4,128,256]{2,1,0:T(8,128)(2,1)} %get-tuple-element.65.attn_ref, bf16[4,8,128,512]{3,2,1,0:T(8,128)(2,1)} %get-tuple-element.66.ffn_whole), custom_call_target="tpu_custom_call" | custom-call | tf_op jit(solution)/shard_map/newton_schulz/pallas_call | solution.py:505
  384.3 0.0 copy-start.1
  384.3 0.0 copy-start
  384.3 5.7 %update.1 = (f32[4,128,256]{2,1,0:T(8,128)}, f32[2,128,1024]{2,1,0:T(8,128)}, f32[12,32]{1,0:T(8,128)}, f32[4,128,256]{2,1,0:T(8,128)}, f32[2,128,1024]{2,1,0:T(...) custom-call(f32[4,128,256]{2,1,0:T(8,128)} %attn_w.3, ...), custom_call_target="tpu_custom_call" | custom-call | tf_op jit(solution)/shard_map/update/pallas_call | solution.py:602
  390.0 1.3 dynamic-slice_bitcast_fusion
  391.2 0.0 copy-done.1
  391.2 1.0 copy.26
  392.2 0.0 copy-done
  392.2 1.3 copy.27
Async XLA Ops:
  384.3 6.9 %copy-start.1 = (bf16[512,1024]{1,0:T(8,128)(2,1)S(1)}, bf16[512,1024]{1,0:T(8,128)(2,1)}, u32[]{:S(2)}) copy-start(bf16[512,1024]{1,0:T(8,128)(2,1)} %get-tuple-element.90) | copy-start | bytes 3145732
  384.3 7.9 %copy-start = (f32[512,1024]{1,0:T(8,128)S(1)}, f32[512,1024]{1,0:T(8,128)}, u32[]{:S(2)}) copy-start(f32[512,1024]{1,0:T(8,128)} %get-tuple-element.91) | copy-start | bytes 6291460
